TPU v7x, 128 devices: a whole 4x4x4 slice. The times are simulated.
128 devices in a mesh: ia: 4 (over z), ja: 8 (over y_lo, x), ka: 4 (over y_hi, core).
Axes of the slice: x: 4, y: 4 (y_hi: 2, y_lo: 2; y = y_hi * 2 + y_lo), z: 4, core: 2. Of those that a mesh axis runs over, the one named last changes fastest.
Arguments:
- inputs: bfloat16 [2048, 6144], P(('ia', 'ka'), 'ja'), may hold values from -6 to 6
- up_weight: bfloat16 [6144, 24576], P('ja', ('ka', 'ia')), may hold values from -0.078125 to 0.078125
- down_weight: bfloat16 [24576, 6144], P(('ka', 'ia'), 'ja'), may hold values from -0.0390625 to 0.0390625
- out_grad: bfloat16 [2048, 6144], P(('ia', 'ka'), 'ja'), may hold values from -1.1953125 to 1.1953125
Outputs:
- output: bfloat16 [2048, 6144], P(('ia', 'ka'), 'ja')
- input_grad: bfloat16 [2048, 6144], P(('ia', 'ka'), 'ja')
- up_grad: bfloat16 [6144, 24576], P('ja', ('ka', 'ia'))
- down_grad: bfloat16 [24576, 6144], P(('ka', 'ia'), 'ja')
All inputs are finite; a program needn't handle non-finite values.
Results may differ from a plain program's by a relative error of at most 0.025.
Values may be sent and summed in bfloat16 or wider, within the bound.
A program may use at most 128 MiB of HBM per device.

v0:
```python
import jax
import jax.numpy as jnp
from jax import lax
from jax.sharding import PartitionSpec as P

sqrt_two_over_pi = 0.7978845608028654
cubic_coeff = 0.044715


def gelu_value(preact):
    tanh_inner = jnp.tanh(sqrt_two_over_pi * (preact + cubic_coeff * preact * preact * preact))
    return 0.5 * preact * (1.0 + tanh_inner)


def gelu_slope(preact):
    tanh_inner = jnp.tanh(sqrt_two_over_pi * (preact + cubic_coeff * preact * preact * preact))
    inner_slope = sqrt_two_over_pi * (1.0 + 3.0 * cubic_coeff * preact * preact)
    return 0.5 * (1.0 + tanh_inner) + 0.5 * preact * (1.0 - tanh_inner * tanh_inner) * inner_slope


def contract_rows(left, right):
    return lax.dot_general(
        left, right, (((0,), (0,)), ((), ())), preferred_element_type=jnp.float32
    )


def contract_cols(left, right):
    return lax.dot_general(
        left, right, (((1,), (1,)), ((), ())), preferred_element_type=jnp.float32
    )


def per_device(inputs, up_weight, down_weight, out_grad):
    token_in, grad_in = (
        lax.all_gather(inputs, "ka", axis=0, tiled=True),
        lax.all_gather(out_grad, "ka", axis=0, tiled=True),
    )
    up_full = lax.all_gather(up_weight, "ia", axis=1, tiled=True)
    preact_part = jnp.dot(token_in, up_full, preferred_element_type=jnp.float32)
    preact = lax.psum_scatter(
        preact_part.astype(jnp.bfloat16), "ja", scatter_dimension=0, tiled=True
    ).astype(jnp.float32)
    hidden = lax.all_gather(gelu_value(preact).astype(jnp.bfloat16), "ja", axis=0, tiled=True)
    weight_piece = lax.all_gather(down_weight, "ia", axis=0, tiled=True)
    hidden_cols = hidden
    output_part = jnp.dot(hidden_cols, weight_piece, preferred_element_type=jnp.float32)
    grad_block = contract_cols(grad_in, weight_piece)
    grad_part = grad_block
    output_part, grad_part = (output_part, grad_part)
    output = lax.psum_scatter(
        output_part.astype(jnp.bfloat16), "ka", scatter_dimension=0, tiled=True
    )
    hidden_grad = lax.psum_scatter(
        grad_part.astype(jnp.bfloat16), "ja", scatter_dimension=0, tiled=True
    ).astype(jnp.float32)
    preact_grad = lax.all_gather(
        (hidden_grad * gelu_slope(preact)).astype(jnp.bfloat16), "ja", axis=0, tiled=True
    )
    input_part = contract_cols(preact_grad, up_full)
    input_grad = lax.psum_scatter(
        input_part.astype(jnp.bfloat16), "ka", scatter_dimension=0, tiled=True
    )
    up_rows = lax.psum_scatter(
        contract_rows(preact_grad, token_in).astype(jnp.bfloat16),
        "ia",
        scatter_dimension=0,
        tiled=True,
    ).astype(jnp.float32)
    hidden_cols = hidden
    down_rows = lax.psum_scatter(
        contract_rows(hidden_cols, grad_in).astype(jnp.bfloat16),
        "ia",
        scatter_dimension=0,
        tiled=True,
    )
    up_grad = up_rows.T.astype(jnp.bfloat16)
    return (output, input_grad, up_grad, down_rows)


def solution(mesh):
    placed = (
        P(("ia", "ka"), "ja"),
        P("ja", ("ka", "ia")),
        P(("ka", "ia"), "ja"),
        P(("ia", "ka"), "ja"),
    )
    return jax.shard_map(
        per_device,
        mesh=mesh,
        in_specs=placed,
        out_specs=(
            P(("ia", "ka"), "ja"),
            P(("ia", "ka"), "ja"),
            P("ja", ("ka", "ia")),
            P(("ka", "ia"), "ja"),
        ),
        check_vma=False,
    )
```

profile of v0, /device:TPU:0, one launch (start us, length us, event | category | flops | bytes accessed | tf_op | source)
XLA Modules:
  0.0 752.1 jit_solution(5770281442656845434)
XLA Ops:
  7.2 0.7 all-gather.9.cloned.1.call-update
  7.9 0.7 all-gather.5.cloned.1.call-update
  8.6 0.0 reduce-scatter.11.cloned.1.call-start
  8.7 10.6 %all_gather.22 = bf16[512,768]{1,0:T(8,128)(2,1)S(1)} all-gather(bf16[128,768]{1,0:T(8,128)(2,1)} %param.7), channel_id=1, replica_groups=mesh['ia'=4,'ja'=8,'ka'=4] {'ka'}, dimensions={0}, use_global_device_ids=true | all-gather | bytes 983040 | tf_op jit(solution)/shard_map/all_gather | solution.py:36
  19.3 84.9 %all-gather.9.cloned.1.call-done = bf16[6144,768]{1,0:T(8,128)(2,1)} async-done(((bf16[1536,768]{1,0:T(8,128)(2,1)}), bf16[6144,768]{1,0:T(8,128)(2,1)}) %all-gather.9.cloned.1.call-update) | async-done | bytes 9437200 | tf_op jit(solution)/shard_map/all_gather | solution.py:44
  104.2 10.6 %convolution_convert_fusion.2 = bf16[512,6144]{1,0:T(8,128)(2,1)} fusion(bf16[512,768]{1,0:T(8,128)(2,1)S(1)} %all_gather.22, bf16[6144,768]{1,0:T(8,128)(2,1)} %all-gather.9.cloned.1.call-done), kind=kOutput, calls=%fused_computation.2 | convolution fusion | flops 4834983936 | bytes 16515072 | tf_op jit(solution)/shard_map/dot_general | solution.py:28
  114.9 0.0 reduce-scatter.7.cloned.1.call-start
  114.9 0.9 copy-done
  115.8 10.1 %all_gather.18 = bf16[512,768]{1,0:T(8,128)(2,1)S(1)} all-gather(bf16[128,768]{1,0:T(8,128)(2,1)S(1)} %copy-done), channel_id=1, replica_groups=mesh['ia'=4,'ja'=8,'ka'=4] {'ka'}, dimensions={0}, use_global_device_ids=true | all-gather | bytes 983040 | tf_op jit(solution)/shard_map/all_gather | solution.py:35
  125.9 73.0 %all-gather.5.cloned.1.call-done = bf16[768,6144]{1,0:T(8,128)(2,1)} async-done(((bf16[768,1536]{1,0:T(8,128)(2,1)}), bf16[768,6144]{1,0:T(8,128)(2,1)}) %all-gather.5.cloned.1.call-update) | async-done | bytes 9437200 | tf_op jit(solution)/shard_map/all_gather | solution.py:38
  198.9 10.6 %convolution_convert_fusion.3 = bf16[512,6144]{1,0:T(8,128)(2,1)} fusion(bf16[512,768]{1,0:T(8,128)(2,1)S(1)} %all_gather.18, bf16[768,6144]{1,0:T(8,128)(2,1)} %all-gather.5.cloned.1.call-done), kind=kOutput, calls=%fused_computation.3 | convolution fusion | flops 4834983936 | bytes 16515072 | tf_op jit(solution)/shard_map/dot_general | solution.py:39
  209.6 0.0 all-gather.11.cloned.1.call-start
  209.7 65.5 %reduce-scatter.11.cloned.1.call-done = bf16[64,6144]{1,0:T(8,128)(2,1)} async-done(((bf16[512,6144]{1,0:T(8,128)(2,1)}), bf16[64,6144]{1,0:T(8,128)(2,1)}) %reduce-scatter.11.cloned.1.call-update) | async-done | bytes 786448 | tf_op jit(solution)/shard_map/reduce_scatter | solution.py:53
  275.2 74.0 %reduce-scatter.7.cloned.1.call-done = bf16[64,6144]{1,0:T(8,128)(2,1)} async-done(((bf16[512,6144]{1,0:T(8,128)(2,1)}), bf16[64,6144]{1,0:T(8,128)(2,1)}) %reduce-scatter.7.cloned.1.call-update) | async-done | bytes 786448 | tf_op jit(solution)/shard_map/reduce_scatter | solution.py:40
  349.2 3.7 fusion.6
  352.9 0.0 all-gather.7.cloned.1.call-start
  352.9 0.5 all-gather.7.cloned.1.call-update
  353.4 0.0 reduce-scatter.15.cloned.1.call-start
  353.5 70.6 %all-gather.11.cloned.1.call-done = bf16[512,6144]{1,0:T(8,128)(2,1)} async-done(((bf16[64,6144]{1,0:T(8,128)(2,1)}), bf16[512,6144]{1,0:T(8,128)(2,1)}) %all-gather.11.cloned.1.call-update) | async-done | bytes 6291472 | tf_op jit(solution)/shard_map/all_gather | solution.py:56
  424.1 10.3 %convolution_convert_fusion.1 = bf16[6144,768]{1,0:T(8,128)(2,1)} fusion(bf16[512,6144]{1,0:T(8,128)(2,1)} %all-gather.11.cloned.1.call-done, bf16[512,768]{1,0:T(8,128)(2,1)S(1)} %all_gather.18), kind=kOutput, calls=%fused_computation.1 | convolution fusion | flops 4836556800 | bytes 16515072 | tf_op jit(solution)/shard_map/dot_general | solution.py:22
  434.4 0.0 reduce-scatter.13.cloned.1.call-start
  434.5 10.7 %convolution_convert_fusion.4 = bf16[512,768]{1,0:T(8,128)(2,1)} fusion(bf16[512,6144]{1,0:T(8,128)(2,1)} %all-gather.11.cloned.1.call-done, bf16[768,6144]{1,0:T(8,128)(2,1)} %all-gather.5.cloned.1.call-done), kind=kOutput, calls=%fused_computation.22 | convolution fusion | flops 4832231424 | bytes 16515072 | tf_op jit(solution)/shard_map/dot_general | solution.py:28
  445.2 0.2 reduce-scatter.9.cloned.1.call-start
  445.4 51.8 %all-gather.7.cloned.1.call-done = bf16[512,6144]{1,0:T(8,128)(2,1)} async-done(((bf16[64,6144]{1,0:T(8,128)(2,1)}), bf16[512,6144]{1,0:T(8,128)(2,1)}) %all-gather.7.cloned.1.call-update) | async-done | bytes 6291472 | tf_op jit(solution)/shard_map/all_gather | solution.py:43
  497.2 10.6 %convolution_convert_fusion.5 = bf16[512,768]{1,0:T(8,128)(2,1)} fusion(bf16[512,6144]{1,0:T(8,128)(2,1)} %all-gather.7.cloned.1.call-done, bf16[6144,768]{1,0:T(8,128)(2,1)} %all-gather.9.cloned.1.call-done), kind=kOutput, calls=%fused_computation.23 | convolution fusion | flops 4832231424 | bytes 16515072 | tf_op jit(solution)/shard_map/dot_general | solution.py:46
  507.8 0.0 reduce-scatter.17.cloned.1.call-start
  507.9 10.4 %convolution_convert_fusion = bf16[6144,768]{1,0:T(8,128)(2,1)} fusion(bf16[512,6144]{1,0:T(8,128)(2,1)} %all-gather.7.cloned.1.call-done, bf16[512,768]{1,0:T(8,128)(2,1)S(1)} %all_gather.22), kind=kOutput, calls=%fused_computation | convolution fusion | flops 4836556800 | bytes 16515072 | tf_op jit(solution)/shard_map/dot_general | solution.py:22
  518.3 69.4 %reduce-scatter.15.cloned.1.call-done = bf16[1536,768]{1,0:T(8,128)(2,1)} async-done(((bf16[6144,768]{1,0:T(8,128)(2,1)}), bf16[1536,768]{1,0:T(8,128)(2,1)}) %reduce-scatter.15.cloned.1.call-update) | async-done | bytes 2359312 | tf_op jit(solution)/shard_map/reduce_scatter | solution.py:63
  587.7 4.3 copy.8
  592.0 28.8 %reduce-scatter.13.cloned.1.call-done = bf16[128,768]{1,0:T(8,128)(2,1)} async-done(((bf16[512,768]{1,0:T(8,128)(2,1)}), bf16[128,768]{1,0:T(8,128)(2,1)}) %reduce-scatter.13.cloned.1.call-update) | async-done | bytes 196624 | tf_op jit(solution)/shard_map/reduce_scatter | solution.py:60
  620.7 33.0 %reduce-scatter.9.cloned.1.call-done = bf16[128,768]{1,0:T(8,128)(2,1)} async-done(((bf16[512,768]{1,0:T(8,128)(2,1)}), bf16[128,768]{1,0:T(8,128)(2,1)}) %reduce-scatter.9.cloned.1.call-update) | async-done | bytes 196624 | tf_op jit(solution)/shard_map/reduce_scatter | solution.py:50
  653.7 91.5 %reduce-scatter.17.cloned.1.call-done = bf16[1536,768]{1,0:T(8,128)(2,1)} async-done(((bf16[6144,768]{1,0:T(8,128)(2,1)}), bf16[1536,768]{1,0:T(8,128)(2,1)}) %reduce-scatter.17.cloned.1.call-update) | async-done | bytes 2359312 | tf_op jit(solution)/shard_map/reduce_scatter | solution.py:70
  (10 shorter events, 0.2 us)
Async XLA Ops:
  7.2 97.1 %all-gather.9.cloned.1.call-start = ((), (), s32[]{:S(2)}) async-start(), calls=%async_computation.9 | async-start | bytes 11796480 | tf_op jit(solution)/shard_map/all_gather | solution.py:44
  7.9 191.0 %all-gather.5.cloned.1.call-start = ((), (), s32[]{:S(2)}) async-start(), calls=%async_computation.6 | async-start | bytes 11796480 | tf_op jit(solution)/shard_map/all_gather | solution.py:38
  8.6 266.5 %reduce-scatter.11.cloned.1.call-start = ((), (), s32[]{:S(2)}) async-start(), calls=%async_computation.11 | async-start | bytes 7077888 | tf_op jit(solution)/shard_map/reduce_scatter | solution.py:53
  114.9 1.0 copy-start
  114.9 234.3 %reduce-scatter.7.cloned.1.call-start = ((), (), s32[]{:S(2)}) async-start(), calls=%async_computation.7 | async-start | bytes 7077888 | tf_op jit(solution)/shard_map/reduce_scatter | solution.py:40
  209.6 214.5 %all-gather.11.cloned.1.call-start = ((), (), s32[]{:S(2)}) async-start(), calls=%async_computation.12 | async-start | bytes 7077888 | tf_op jit(solution)/shard_map/all_gather | solution.py:56
  352.9 144.3 %all-gather.7.cloned.1.call-start = ((), (), s32[]{:S(2)}) async-start(), calls=%async_computation.8 | async-start | bytes 7077888 | tf_op jit(solution)/shard_map/all_gather | solution.py:43
  353.4 234.3 %reduce-scatter.15.cloned.1.call-start = ((), (), s32[]{:S(2)}) async-start(), calls=%async_computation.14 | async-start | bytes 11796480 | tf_op jit(solution)/shard_map/reduce_scatter | solution.py:63
  434.4 186.3 %reduce-scatter.13.cloned.1.call-start = ((), (), s32[]{:S(2)}) async-start(), calls=%async_computation.13 | async-start | bytes 983040 | tf_op jit(solution)/shard_map/reduce_scatter | solution.py:60
  445.2 208.5 %reduce-scatter.9.cloned.1.call-start = ((), (), s32[]{:S(2)}) async-start(), calls=%async_computation.10 | async-start | bytes 983040 | tf_op jit(solution)/shard_map/reduce_scatter | solution.py:50
  507.8 237.5 %reduce-scatter.17.cloned.1.call-start = ((), (), s32[]{:S(2)}) async-start(), calls=%async_computation.15 | async-start | bytes 11796480 | tf_op jit(solution)/shard_map/reduce_scatter | solution.py:70
Sparse Core Ops, SparseCore 0:
  9.7 94.5 all-gather.8
  105.9 93.0 all-gather.4
  201.4 73.7 reduce-scatter.10
  277.5 71.6 reduce-scatter.6
  353.0 71.0 all-gather.10
  426.2 71.0 all-gather.6
  499.7 87.9 reduce-scatter.14
  590.9 29.7 reduce-scatter.12
  624.1 29.5 reduce-scatter.8
  656.6 88.6 reduce-scatter.16
where the time goes:
time: 753 us; the launch traced here: 752 us
  waiting for transfers between devices  645 us (86%)
  matrix products  63.2 us (8%)
  blocking collectives  20.7 us (3%)
  between operations  14.2 us (2%)
    reduce_scatter x1, waiting for transfers between devices, per_device(): lax.psum_scatter(contract_rows(hidden_cols, grad_in).astype(jnp.bfloat16)...  91.5 us
    all_gather x1, waiting for transfers between devices, per_device(): weight_piece = lax.all_gather(down_weight, 'ia', axis=0, tiled=True)  84.9 us
    reduce_scatter x1, waiting for transfers between devices, per_device(): lax.psum_scatter(preact_part.astype(jnp.bfloat16), 'ja', scatter_dimensio...  74 us
    all_gather x1, waiting for transfers between devices, per_device(): up_full = lax.all_gather(up_weight, 'ia', axis=1, tiled=True)  73 us
    all_gather x1, waiting for transfers between devices, per_device(): lax.all_gather((hidden_grad * gelu_slope(preact)).astype(jnp.bfloat16), '...  70.6 us
    reduce_scatter x1, waiting for transfers between devices, per_device(): lax.psum_scatter(contract_rows(preact_grad, token_in).astype(jnp.bfloat16...  69.4 us
    reduce_scatter x1, waiting for transfers between devices, per_device(): lax.psum_scatter(grad_part.astype(jnp.bfloat16), 'ja', scatter_dimension=...  65.5 us
    all_gather x1, waiting for transfers between devices, per_device(): lax.all_gather(gelu_value(preact).astype(jnp.bfloat16), 'ja', axis=0, til...  51.8 us
  transfers between devices with their start and end apart: 10, of which 10 were waited for; matrix products, arithmetic and copies ran while one was open for 9% of the time, Pallas kernels for 0%

commit v1 on v0

v1 whole, which is shorter than its diff:
```python
import jax
import jax.numpy as jnp
from jax import lax
from jax.sharding import PartitionSpec as P

sqrt_two_over_pi = 0.7978845608028654
cubic_coeff = 0.044715
CHUNKS = 4


def gelu_value(preact):
    tanh_inner = jnp.tanh(sqrt_two_over_pi * (preact + cubic_coeff * preact * preact * preact))
    return 0.5 * preact * (1.0 + tanh_inner)


def gelu_slope(preact):
    tanh_inner = jnp.tanh(sqrt_two_over_pi * (preact + cubic_coeff * preact * preact * preact))
    inner_slope = sqrt_two_over_pi * (1.0 + 3.0 * cubic_coeff * preact * preact)
    return 0.5 * (1.0 + tanh_inner) + 0.5 * preact * (1.0 - tanh_inner * tanh_inner) * inner_slope


def contract_rows(left, right):
    return lax.dot_general(
        left, right, (((0,), (0,)), ((), ())), preferred_element_type=jnp.float32
    )


def contract_cols(left, right):
    return lax.dot_general(
        left, right, (((1,), (1,)), ((), ())), preferred_element_type=jnp.float32
    )


def per_device(inputs, up_weight, down_weight, out_grad):
    tokens = ("ia", "ka")
    token_in = lax.all_gather(inputs, tokens, axis=0, tiled=True)
    grad_in = lax.all_gather(out_grad, tokens, axis=0, tiled=True)

    def forward(rows):
        part = jnp.dot(token_in[rows], up_weight, preferred_element_type=jnp.float32)
        grad = contract_cols(grad_in[rows], down_weight)
        preact = lax.psum_scatter(
            part.astype(jnp.bfloat16), "ja", scatter_dimension=0, tiled=True
        ).astype(jnp.float32)
        hidden_grad = lax.psum_scatter(
            grad.astype(jnp.bfloat16), "ja", scatter_dimension=0, tiled=True
        ).astype(jnp.float32)
        hidden = gelu_value(preact).astype(jnp.bfloat16)
        preact_grad = (hidden_grad * gelu_slope(preact)).astype(jnp.bfloat16)
        return (
            lax.all_gather(hidden, "ja", axis=0, tiled=True),
            lax.all_gather(preact_grad, "ja", axis=0, tiled=True),
        )

    step = token_in.shape[0] // CHUNKS
    pieces = [forward(slice(c * step, (c + 1) * step)) for c in range(CHUNKS)]
    hidden = jnp.concatenate([piece[0] for piece in pieces], axis=0)
    preact_grad = jnp.concatenate([piece[1] for piece in pieces], axis=0)
    output = lax.psum_scatter(
        jnp.dot(hidden, down_weight, preferred_element_type=jnp.float32).astype(jnp.bfloat16),
        tokens, scatter_dimension=0, tiled=True,
    )
    input_grad = lax.psum_scatter(
        contract_cols(preact_grad, up_weight).astype(jnp.bfloat16),
        tokens, scatter_dimension=0, tiled=True,
    )
    up_grad = contract_rows(token_in, preact_grad).astype(jnp.bfloat16)
    down_grad = contract_rows(hidden, grad_in).astype(jnp.bfloat16)
    return (output, input_grad, up_grad, down_grad)


def solution(mesh):
    placed = (
        P(("ia", "ka"), "ja"),
        P("ja", ("ka", "ia")),
        P(("ka", "ia"), "ja"),
        P(("ia", "ka"), "ja"),
    )
    return jax.shard_map(
        per_device,
        mesh=mesh,
        in_specs=placed,
        out_specs=(
            P(("ia", "ka"), "ja"),
            P(("ia", "ka"), "ja"),
            P("ja", ("ka", "ia")),
            P(("ka", "ia"), "ja"),
        ),
        check_vma=False,
    )
```

time: 753 us -> 951 us (1.26)
  waiting for transfers between devices: 645 us -> 831 us
  local copies, waits for them, and re-layouts: 5.16 us -> 26 us
  blocking collectives: 20.7 us -> 0 us
    all_gather x4 -> x10, waiting for transfers between devices: 280 us -> 403 us  [the longest x4 154 us: forward(): lax.all_gather(preact_grad, 'ja', axis=0, tiled=True)]
    reduce_scatter x6 -> x10, waiting for transfers between devices: 362 us -> 424 us  [the longest x4 168 us: forward(): lax.psum_scatter(grad.astype(jnp.bfloat16), 'ja', scatter_dimension=0, ti...]
    all_gather x2 -> x0, blocking collectives: 20.7 us -> none  [the longest x1 10.6 us: per_device(): lax.all_gather(out_grad, 'ka', axis=0, tiled=True)]
    unnamed x3 -> x11, local copies, waits for them, and re-layouts: 5.16 us -> 20.4 us
    dot_general x2 -> x5, matrix products: 21.4 us -> 27.5 us  [contract_cols(): lax.dot_general(left, right, (((1,), (1,)), ((), ())), preferred_element_...]
    dot_general x2 -> x5, matrix products: 21.2 us -> 24.1 us  [the longest x4 14.8 us: forward(): jnp.dot(token_in[rows], up_weight, preferred_element_type=jnp.float32)]
  transfers between devices with their start and end apart: 10 -> 20, of which waited for: 10 -> 20; matrix products, arithmetic and copies ran while one was open for 9% -> 11% of each run, Pallas kernels for 0% -> 0%
where the time goes in v1:
time: 951 us; the launch traced here: 950 us
  waiting for transfers between devices  831 us (87%)
  matrix products  70.2 us (7%)
  local copies, waits for them, and re-layouts  26 us (3%)
  between operations  14.4 us (2%)
    reduce_scatter x4, waiting for transfers between devices, forward(): lax.psum_scatter(grad.astype(jnp.bfloat16), 'ja', scatter_dimension=0, ti...  168 us
    all_gather x4, waiting for transfers between devices, forward(): lax.all_gather(preact_grad, 'ja', axis=0, tiled=True)  154 us
    all_gather x4, waiting for transfers between devices, forward(): lax.all_gather(hidden, 'ja', axis=0, tiled=True)  146 us
    reduce_scatter x4, waiting for transfers between devices, forward(): lax.psum_scatter(part.astype(jnp.bfloat16), 'ja', scatter_dimension=0, ti...  133 us
    reduce_scatter x1, waiting for transfers between devices, per_device(): lax.psum_scatter(jnp.dot(hidden, down_weight, preferred_element_type=jnp....  78.8 us
    all_gather x1, waiting for transfers between devices, per_device(): token_in = lax.all_gather(inputs, tokens, axis=0, tiled=True)  55.2 us
    all_gather x1, waiting for transfers between devices, per_device(): grad_in = lax.all_gather(out_grad, tokens, axis=0, tiled=True)  48.3 us
    reduce_scatter x1, waiting for transfers between devices, per_device(): lax.psum_scatter(contract_cols(preact_grad, up_weight).astype(jnp.bfloat1...  44.2 us
  transfers between devices with their start and end apart: 20, of which 20 were waited for; matrix products, arithmetic and copies ran while one was open for 11% of the time, Pallas kernels for 0%

profile of v1, /device:TPU:0, one launch (start us, length us, event | category | flops | bytes accessed | tf_op | source)
XLA Modules:
  0.0 950.4 jit_solution(4795945013525612297)
XLA Ops:
  8.7 55.2 %all-gather.11.cloned.1.call-done = bf16[2048,768]{1,0:T(8,128)(2,1)} async-done(((bf16[128,768]{1,0:T(8,128)(2,1)}), bf16[2048,768]{1,0:T(8,128)(2,1)}) %all-gather.11.cloned.1.call-update) | async-done | bytes 3145744 | tf_op jit(solution)/shard_map/all_gather | solution.py:36
  67.6 48.3 %all-gather.21.cloned.1.call-done = bf16[2048,768]{1,0:T(8,128)(2,1)} async-done(((bf16[128,768]{1,0:T(8,128)(2,1)}), bf16[2048,768]{1,0:T(8,128)(2,1)}) %all-gather.21.cloned.1.call-update) | async-done | bytes 3145744 | tf_op jit(solution)/shard_map/all_gather | solution.py:37
  115.9 4.5 convolution_convert_fusion.7
  120.5 3.7 convolution_convert_fusion.10
  124.3 4.6 convolution_convert_fusion.6
  128.9 3.7 convolution_convert_fusion.9
  132.7 4.5 convolution_convert_fusion.5
  137.3 3.7 convolution_convert_fusion.8
  141.0 4.5 convolution_convert_fusion.4
  145.6 12.8 %reduce-scatter.11.cloned.1.call-done = bf16[64,1536]{1,0:T(8,128)(2,1)} async-done(((bf16[512,1536]{1,0:T(8,128)(2,1)}), bf16[64,1536]{1,0:T(8,128)(2,1)}) %reduce-scatter.11.cloned.1.call-update) | async-done | bytes 196624 | tf_op jit(solution)/shard_map/reduce_scatter | solution.py:42
  158.5 42.5 %reduce-scatter.21.cloned.1.call-done = bf16[64,1536]{1,0:T(8,128)(2,1)} async-done(((bf16[512,1536]{1,0:T(8,128)(2,1)}), bf16[64,1536]{1,0:T(8,128)(2,1)}) %reduce-scatter.21.cloned.1.call-update) | async-done | bytes 196624 | tf_op jit(solution)/shard_map/reduce_scatter | solution.py:45
  203.1 39.8 %reduce-scatter.13.cloned.1.call-done = bf16[64,1536]{1,0:T(8,128)(2,1)} async-done(((bf16[512,1536]{1,0:T(8,128)(2,1)}), bf16[64,1536]{1,0:T(8,128)(2,1)}) %reduce-scatter.13.cloned.1.call-update) | async-done | bytes 196624 | tf_op jit(solution)/shard_map/reduce_scatter | solution.py:42
  242.9 41.9 %reduce-scatter.23.cloned.1.call-done = bf16[64,1536]{1,0:T(8,128)(2,1)} async-done(((bf16[512,1536]{1,0:T(8,128)(2,1)}), bf16[64,1536]{1,0:T(8,128)(2,1)}) %reduce-scatter.23.cloned.1.call-update) | async-done | bytes 196624 | tf_op jit(solution)/shard_map/reduce_scatter | solution.py:45
  287.0 40.0 %reduce-scatter.15.cloned.1.call-done = bf16[64,1536]{1,0:T(8,128)(2,1)} async-done(((bf16[512,1536]{1,0:T(8,128)(2,1)}), bf16[64,1536]{1,0:T(8,128)(2,1)}) %reduce-scatter.15.cloned.1.call-update) | async-done | bytes 196624 | tf_op jit(solution)/shard_map/reduce_scatter | solution.py:42
  327.0 42.0 %reduce-scatter.25.cloned.1.call-done = bf16[64,1536]{1,0:T(8,128)(2,1)} async-done(((bf16[512,1536]{1,0:T(8,128)(2,1)}), bf16[64,1536]{1,0:T(8,128)(2,1)}) %reduce-scatter.25.cloned.1.call-update) | async-done | bytes 196624 | tf_op jit(solution)/shard_map/reduce_scatter | solution.py:45
  371.2 40.0 %reduce-scatter.17.cloned.1.call-done = bf16[64,1536]{1,0:T(8,128)(2,1)} async-done(((bf16[512,1536]{1,0:T(8,128)(2,1)}), bf16[64,1536]{1,0:T(8,128)(2,1)}) %reduce-scatter.17.cloned.1.call-update) | async-done | bytes 196624 | tf_op jit(solution)/shard_map/reduce_scatter | solution.py:42
  411.2 41.9 %reduce-scatter.27.cloned.1.call-done = bf16[64,1536]{1,0:T(8,128)(2,1)} async-done(((bf16[512,1536]{1,0:T(8,128)(2,1)}), bf16[64,1536]{1,0:T(8,128)(2,1)}) %reduce-scatter.27.cloned.1.call-update) | async-done | bytes 196624 | tf_op jit(solution)/shard_map/reduce_scatter | solution.py:45
  457.6 37.1 %all-gather.23.cloned.1.call-done = bf16[512,1536]{1,0:T(8,128)(2,1)} async-done(((bf16[64,1536]{1,0:T(8,128)(2,1)}), bf16[512,1536]{1,0:T(8,128)(2,1)}) %all-gather.23.cloned.1.call-update) | async-done | bytes 1572880 | tf_op jit(solution)/shard_map/all_gather | solution.py:52
  497.3 39.2 %all-gather.25.cloned.1.call-done = bf16[512,1536]{1,0:T(8,128)(2,1)} async-done(((bf16[64,1536]{1,0:T(8,128)(2,1)}), bf16[512,1536]{1,0:T(8,128)(2,1)}) %all-gather.25.cloned.1.call-update) | async-done | bytes 1572880 | tf_op jit(solution)/shard_map/all_gather | solution.py:52
  539.2 38.7 %all-gather.27.cloned.1.call-done = bf16[512,1536]{1,0:T(8,128)(2,1)} async-done(((bf16[64,1536]{1,0:T(8,128)(2,1)}), bf16[512,1536]{1,0:T(8,128)(2,1)}) %all-gather.27.cloned.1.call-update) | async-done | bytes 1572880 | tf_op jit(solution)/shard_map/all_gather | solution.py:52
  580.6 38.6 %all-gather.29.cloned.1.call-done = bf16[512,1536]{1,0:T(8,128)(2,1)} async-done(((bf16[64,1536]{1,0:T(8,128)(2,1)}), bf16[512,1536]{1,0:T(8,128)(2,1)}) %all-gather.29.cloned.1.call-update) | async-done | bytes 1572880 | tf_op jit(solution)/shard_map/all_gather | solution.py:52
  621.9 9.4 convolution_convert_fusion.2
  631.5 29.5 %all-gather.13.cloned.1.call-done = bf16[512,1536]{1,0:T(8,128)(2,1)} async-done(((bf16[64,1536]{1,0:T(8,128)(2,1)}), bf16[512,1536]{1,0:T(8,128)(2,1)}) %all-gather.13.cloned.1.call-update) | async-done | bytes 1572880 | tf_op jit(solution)/shard_map/all_gather | solution.py:51
  663.7 39.2 %all-gather.15.cloned.1.call-done = bf16[512,1536]{1,0:T(8,128)(2,1)} async-done(((bf16[64,1536]{1,0:T(8,128)(2,1)}), bf16[512,1536]{1,0:T(8,128)(2,1)}) %all-gather.15.cloned.1.call-update) | async-done | bytes 1572880 | tf_op jit(solution)/shard_map/all_gather | solution.py:51
  705.5 38.6 %all-gather.17.cloned.1.call-done = bf16[512,1536]{1,0:T(8,128)(2,1)} async-done(((bf16[64,1536]{1,0:T(8,128)(2,1)}), bf16[512,1536]{1,0:T(8,128)(2,1)}) %all-gather.17.cloned.1.call-update) | async-done | bytes 1572880 | tf_op jit(solution)/shard_map/all_gather | solution.py:51
  746.8 38.6 %all-gather.19.cloned.1.call-done = bf16[512,1536]{1,0:T(8,128)(2,1)} async-done(((bf16[64,1536]{1,0:T(8,128)(2,1)}), bf16[512,1536]{1,0:T(8,128)(2,1)}) %all-gather.19.cloned.1.call-update) | async-done | bytes 1572880 | tf_op jit(solution)/shard_map/all_gather | solution.py:51
  788.3 9.3 convolution_convert_fusion.3
  797.6 9.4 fusion
  807.1 4.3 copy.8
  811.4 9.2 convolution_convert_fusion
  820.7 44.2 %reduce-scatter.29.cloned.1.call-done = bf16[128,768]{1,0:T(8,128)(2,1)} async-done(((bf16[2048,768]{1,0:T(8,128)(2,1)}), bf16[128,768]{1,0:T(8,128)(2,1)}) %reduce-scatter.29.cloned.1.call-update) | async-done | bytes 196624 | tf_op jit(solution)/shard_map/reduce_scatter | solution.py:63
  864.8 78.8 %reduce-scatter.19.cloned.1.call-done = bf16[128,768]{1,0:T(8,128)(2,1)} async-done(((bf16[2048,768]{1,0:T(8,128)(2,1)}), bf16[128,768]{1,0:T(8,128)(2,1)}) %reduce-scatter.19.cloned.1.call-update) | async-done | bytes 196624 | tf_op jit(solution)/shard_map/reduce_scatter | solution.py:59
  (57 shorter events, 38.3 us)
Async XLA Ops:
  7.2 56.7 %copy-start = (bf16[768,1536]{1,0:T(8,128)(2,1)S(1)}, bf16[768,1536]{1,0:T(8,128)(2,1)}, u32[]{:S(2)}) copy-start(bf16[768,1536]{1,0:T(8,128)(2,1)} %param.5) | copy-start | bytes 7077892
  7.2 56.7 %all-gather.11.cloned.1.call-start = ((), (), s32[]{:S(2)}) async-start(), calls=%async_computation.10 | async-start | bytes 3342336 | tf_op jit(solution)/shard_map/all_gather | solution.py:36
  7.9 108.0 %all-gather.21.cloned.1.call-start = ((), (), s32[]{:S(2)}) async-start(), calls=%async_computation.20 | async-start | bytes 3342336 | tf_op jit(solution)/shard_map/all_gather | solution.py:37
  8.7 149.8 %reduce-scatter.11.cloned.1.call-start = ((), (), s32[]{:S(2)}) async-start(), calls=%async_computation.11 | async-start | bytes 1769472 | tf_op jit(solution)/shard_map/reduce_scatter | solution.py:42
  67.6 133.4 %reduce-scatter.21.cloned.1.call-start = ((), (), s32[]{:S(2)}) async-start(), calls=%async_computation.21 | async-start | bytes 1769472 | tf_op jit(solution)/shard_map/reduce_scatter | solution.py:45
  120.4 122.5 %reduce-scatter.13.cloned.1.call-start = ((), (), s32[]{:S(2)}) async-start(), calls=%async_computation.13 | async-start | bytes 1769472 | tf_op jit(solution)/shard_map/reduce_scatter | solution.py:42
  124.2 160.7 %reduce-scatter.23.cloned.1.call-start = ((), (), s32[]{:S(2)}) async-start(), calls=%async_computation.23 | async-start | bytes 1769472 | tf_op jit(solution)/shard_map/reduce_scatter | solution.py:45
  128.9 198.1 %reduce-scatter.15.cloned.1.call-start = ((), (), s32[]{:S(2)}) async-start(), calls=%async_computation.15 | async-start | bytes 1769472 | tf_op jit(solution)/shard_map/reduce_scatter | solution.py:42
  132.6 236.4 %reduce-scatter.25.cloned.1.call-start = ((), (), s32[]{:S(2)}) async-start(), calls=%async_computation.25 | async-start | bytes 1769472 | tf_op jit(solution)/shard_map/reduce_scatter | solution.py:45
  137.2 273.9 %reduce-scatter.17.cloned.1.call-start = ((), (), s32[]{:S(2)}) async-start(), calls=%async_computation.17 | async-start | bytes 1769472 | tf_op jit(solution)/shard_map/reduce_scatter | solution.py:42
  141.0 312.1 %reduce-scatter.27.cloned.1.call-start = ((), (), s32[]{:S(2)}) async-start(), calls=%async_computation.27 | async-start | bytes 1769472 | tf_op jit(solution)/shard_map/reduce_scatter | solution.py:45
  145.6 349.1 %all-gather.23.cloned.1.call-start = ((), (), s32[]{:S(2)}) async-start(), calls=%async_computation.22 | async-start | bytes 1769472 | tf_op jit(solution)/shard_map/all_gather | solution.py:52
  203.1 333.4 %all-gather.25.cloned.1.call-start = ((), (), s32[]{:S(2)}) async-start(), calls=%async_computation.24 | async-start | bytes 1769472 | tf_op jit(solution)/shard_map/all_gather | solution.py:52
  287.0 290.9 %all-gather.27.cloned.1.call-start = ((), (), s32[]{:S(2)}) async-start(), calls=%async_computation.26 | async-start | bytes 1769472 | tf_op jit(solution)/shard_map/all_gather | solution.py:52
  371.1 248.1 %all-gather.29.cloned.1.call-start = ((), (), s32[]{:S(2)}) async-start(), calls=%async_computation.28 | async-start | bytes 1769472 | tf_op jit(solution)/shard_map/all_gather | solution.py:52
  455.2 205.8 %all-gather.13.cloned.1.call-start = ((), (), s32[]{:S(2)}) async-start(), calls=%async_computation.12 | async-start | bytes 1769472 | tf_op jit(solution)/shard_map/all_gather | solution.py:51
  455.8 247.1 %all-gather.15.cloned.1.call-start = ((), (), s32[]{:S(2)}) async-start(), calls=%async_computation.14 | async-start | bytes 1769472 | tf_op jit(solution)/shard_map/all_gather | solution.py:51
  456.4 287.8 %all-gather.17.cloned.1.call-start = ((), (), s32[]{:S(2)}) async-start(), calls=%async_computation.16 | async-start | bytes 1769472 | tf_op jit(solution)/shard_map/all_gather | solution.py:51
  457.0 328.5 %all-gather.19.cloned.1.call-start = ((), (), s32[]{:S(2)}) async-start(), calls=%async_computation.18 | async-start | bytes 1769472 | tf_op jit(solution)/shard_map/all_gather | solution.py:51
  457.5 407.3 %reduce-scatter.29.cloned.1.call-start = ((), (), s32[]{:S(2)}) async-start(), calls=%async_computation.29 | async-start | bytes 3342336 | tf_op jit(solution)/shard_map/reduce_scatter | solution.py:63
  631.3 312.3 %reduce-scatter.19.cloned.1.call-start = ((), (), s32[]{:S(2)}) async-start(), calls=%async_computation.19 | async-start | bytes 3342336 | tf_op jit(solution)/shard_map/reduce_scatter | solution.py:59
  785.4 2.9 copy-start.1
Sparse Core Ops, SparseCore 0:
  10.5 53.3 all-gather.10
  66.3 49.5 all-gather.20
  118.9 39.5 reduce-scatter.10
  161.3 39.6 reduce-scatter.20
  203.3 39.6 reduce-scatter.12
  245.2 39.6 reduce-scatter.22
  287.3 39.6 reduce-scatter.14
  329.4 39.5 reduce-scatter.24
  371.4 39.6 reduce-scatter.16
  413.4 39.6 reduce-scatter.26
  455.3 39.2 all-gather.22
  496.7 39.7 all-gather.24
  538.1 39.7 all-gather.26
  579.4 39.7 all-gather.28
  621.3 39.7 all-gather.12
  663.1 39.7 all-gather.14
  704.4 39.7 all-gather.16
  745.6 39.7 all-gather.18
  790.0 74.7 reduce-scatter.28
  869.3 74.2 reduce-scatter.18

commit v2 on v1

v2 whole, which is shorter than its diff:
```python
import functools

import jax
import jax.numpy as jnp
from jax import lax
from jax.experimental import pallas as pl
from jax.experimental.pallas import tpu as pltpu
from jax.sharding import PartitionSpec as P

sqrt_two_over_pi = 0.7978845608028654
cubic_coeff = 0.044715

MESH = pl.DeviceIdType.MESH
BF16 = jnp.bfloat16
F32 = jnp.float32

CHUNKS = 8
SLOTS = 4
WIDE = 1024

NAMES = (
    "tok_y", "tok_z_up", "tok_z_down", "tok_z0", "tok_z1", "tok_core",
    "a_t0", "a_t1", "a_d0", "a_d1", "a_s0", "a_s1", "a_y",
    "b_t0", "b_t1", "b_d0", "b_d1", "b_s0", "b_s1", "b_y",
    "ga_y", "ga_up", "ga_down", "ga_x0", "ga_x1",
    "gb_y", "gb_up", "gb_down", "gb_x0", "gb_x1",
    "o_core", "o_t0", "o_t1", "o_d0", "o_d1", "o_s0", "o_s1", "o_y",
)
INDEX = {name: place for place, name in enumerate(NAMES)}


def gelu_pair(preact):
    tanh_inner = jnp.tanh(sqrt_two_over_pi * (preact + cubic_coeff * preact * preact * preact))
    inner_slope = sqrt_two_over_pi * (1.0 + 3.0 * cubic_coeff * preact * preact)
    value = 0.5 * preact * (1.0 + tanh_inner)
    slope = 0.5 * (1.0 + tanh_inner) + 0.5 * preact * (1.0 - tanh_inner * tanh_inner) * inner_slope
    return value, slope


def contract(left, right, dims):
    return lax.dot_general(left, right, (dims, ((), ())), preferred_element_type=F32)


def kernel(
    x_ref, u_ref, w_ref, g_ref, out_ref, ing_ref, du_ref, dw_ref,
    tok, pa, pb, ta, da, sa, ya_out, ya_in, ya_own, rb, tb, db, sb, ha, hb,
    part, cr, tz, dz, sz, yo_out, yo_in, yo_own, acc_u, acc_w, send_sem, recv_sem,
):
    z0 = lax.axis_index("ia")
    ja = lax.axis_index("ja")
    ka = lax.axis_index("ka")
    y0, x0 = ja // 4, ja % 4
    h0, c0 = ka // 2, ka % 2
    rows = x_ref.shape[0] // CHUNKS

    def at_x(step):
        return (z0, y0 * 4 + (x0 + step + 4) % 4, ka)

    def at_z(step):
        return ((z0 + step + 4) % 4, ja, ka)

    y_pair = (z0, (1 - y0) * 4 + x0, ka)
    h_pair = (z0, ja, (1 - h0) * 2 + c0)
    c_pair = (z0, ja, h0 * 2 + 1 - c0)
    ways = ((0, 1), (1, -1))

    barrier = pltpu.get_barrier_semaphore()
    for other in (at_x(1), at_x(-1), at_z(1), at_z(-1), y_pair, h_pair, c_pair):
        pl.semaphore_signal(barrier, inc=1, device_id=other, device_id_type=MESH)
    for c in range(CHUNKS):
        tok[0, c, c0, z0, h0] = x_ref[c * rows:(c + 1) * rows]
        tok[1, c, c0, z0, h0] = g_ref[c * rows:(c + 1) * rows]
    acc_u[...] = jnp.zeros_like(acc_u)
    acc_w[...] = jnp.zeros_like(acc_w)
    pl.semaphore_wait(barrier, 7)

    def copy(name, c, src, dst, to):
        return pltpu.make_async_remote_copy(
            src_ref=src, dst_ref=dst,
            send_sem=send_sem.at[INDEX[name], c], recv_sem=recv_sem.at[INDEX[name], c],
            device_id=to, device_id_type=MESH,
        )

    def gather_first(name, c, ref_of, mine, to):
        return (
            copy(name + "_up", c, ref_of(mine), ref_of(mine), to(1)),
            copy(name + "_down", c, ref_of(mine), ref_of(mine), to(-1)),
        )

    def gather_second(name, c, ref_of, mine, to, axis):
        return tuple(
            copy(name + "_" + axis + str(t), c, ref_of(t, (mine - way + 4) % 4),
                 ref_of(t, (mine - way + 4) % 4), to(way))
            for t, way in ways
        )

    def sum_far(name, c, t, way, piece, transit, mine, to):
        return copy(f"{name}_t{t}", c, piece(t, (mine + 2) % 4), transit.at[t], to(way))

    def sum_near(name, c, t, way, piece, direct, mine, to):
        return copy(f"{name}_d{t}", c, piece(t, (mine - way + 4) % 4), direct.at[t], to(-way))

    def sum_first(name, c, t, way, piece, transit, direct, mine, to):
        return (
            sum_far(name, c, t, way, piece, transit, mine, to),
            sum_near(name, c, t, way, piece, direct, mine, to),
        )

    def sum_second(name, c, t, way, transit, second, to):
        return copy(f"{name}_s{t}", c, transit.at[t], second.at[t], to(way))

    def sum_middle(name, c, piece, transit, direct, second, mine, to):
        for t, way in ways:
            sum_far(name, c, t, way, piece, transit, mine, to).wait_recv()
            transit[t] = (transit[t].astype(F32) + piece(t, (mine + way + 4) % 4)[...].astype(F32)).astype(BF16)
            sum_second(name, c, t, way, transit, second, to).start()

    def sum_last(name, c, piece, transit, direct, second, mine, to):
        totals = []
        for t, way in ways:
            first, straight = sum_first(name, c, t, way, piece, transit, direct, mine, to)
            straight.wait_recv()
            last = sum_second(name, c, t, way, transit, second, to)
            last.wait_recv()
            first.wait_send()
            straight.wait_send()
            last.wait_send()
            totals.append(
                piece(t, mine)[...].astype(F32) + direct[t].astype(F32) + second[t].astype(F32)
            )
        return totals

    def tok_y(c):
        here = tok.at[:, c, c0, z0, h0]
        return copy("tok_y", c, here, here, h_pair)

    def tok_z(c, z):
        return tok.at[:, c, c0, z]

    def tok_z_one(c, t, z):
        return tok.at[t, c, c0, z]

    def tok_core(c):
        here = tok.at[:, c, c0]
        return copy("tok_core", c, here, here, c_pair)

    def a_piece(c, t, x):
        return pa.at[c % SLOTS, t, x]

    def a_args(c):
        s = c % SLOTS
        return functools.partial(a_piece, c), ta.at[s], da.at[s], sa.at[s], x0, at_x

    def a_y(c):
        s = c % SLOTS
        return copy("a_y", c, ya_out.at[s], ya_in.at[s], y_pair)

    def b_y(c):
        s = c % SLOTS
        return copy("b_y", c, pb.at[s, :, 1 - y0], rb.at[s], y_pair)

    def b_piece(c, t, x):
        return rb.at[c % SLOTS, t, x]

    def b_args(c):
        s = c % SLOTS
        return functools.partial(b_piece, c), tb.at[s], db.at[s], sb.at[s], x0, at_x

    def ga_y(c):
        here = ha.at[:, c, x0, y0]
        return copy("ga_y", c, here, here, y_pair)

    def gb_y(c):
        here = hb.at[:, c, y0]
        return copy("gb_y", c, here, here, y_pair)

    def ga_first(c):
        return gather_first("ga", c, lambda x: ha.at[:, c, x], x0, at_x)

    def ga_second(c):
        return gather_second("ga", c, lambda t, x: ha.at[t, c, x], x0, at_x, "x")

    def gb_first(c):
        return gather_first("gb", c, lambda x: hb.at[:, c, y0, x], x0, at_x)

    def gb_second(c):
        return gather_second("gb", c, lambda t, x: hb.at[t, c, y0, x], x0, at_x, "x")

    def tok_first(c):
        return gather_first("tok_z", c, functools.partial(tok_z, c), z0, at_z)

    def tok_second(c):
        return gather_second("tok", c, functools.partial(tok_z_one, c), z0, at_z, "z")

    def o_core(c):
        return copy("o_core", c, part.at[c % SLOTS, :, 1 - c0], cr.at[c], c_pair)

    def o_args(c):
        return (lambda t, z: cr.at[c, t, z]), tz.at[c], dz.at[c], sz.at[c], z0, at_z

    def o_y(c):
        return copy("o_y", c, yo_out.at[c % SLOTS], yo_in.at[c], h_pair)

    def start(copies):
        for one in copies:
            one.start()

    def finish(copies):
        for one in copies:
            one.wait_recv()
        for one in copies:
            one.wait_send()

    def wide(c, t):
        return tok[t, c].reshape(-1, tok.shape[-1])

    def gather_tokens_first(c):
        finish((tok_y(c),))
        start(tok_first(c))

    def gather_tokens_second(c):
        finish(tok_first(c))
        start(tok_second(c))

    def gather_tokens_core(c):
        finish(tok_second(c))
        start((tok_core(c),))

    def multiply_in(c):
        finish((tok_core(c),))
        s = c % SLOTS
        for t, way in ways:
            if t == 0:
                both = contract(wide(c, 0), u_ref[...], ((1,), (0,)))
            else:
                both = contract(wide(c, 1), w_ref[...], ((1,), (1,)))
            both = both.astype(BF16)
            pa[s, t] = both[:, :WIDE].reshape(pa.shape[2:])
            pb[s, t] = both[:, WIDE:].reshape(pb.shape[2:])
            piece, transit, direct, _, mine, to = a_args(c)
            start(sum_first("a", c, t, way, piece, transit, direct, mine, to))
        b_y(c).start()

    def sum_one(c):
        sum_middle("a", c, *a_args(c))
        b_y(c).wait_recv()
        s = c % SLOTS
        rb[s] = (rb[s].astype(F32) + pb[s, :, y0].astype(F32)).astype(BF16)
        piece, transit, direct, _, mine, to = b_args(c)
        for t, way in ways:
            start(sum_first("b", c, t, way, piece, transit, direct, mine, to))
        b_y(c).wait_send()

    def sum_two(c):
        s = c % SLOTS
        totals = sum_last("a", c, *a_args(c))
        for t in range(2):
            first, second = totals[t][0], totals[t][1]
            ya_own[s, t] = jnp.where(y0 == 0, first, second)
            ya_out[s, t] = jnp.where(y0 == 0, second, first).astype(BF16)
        a_y(c).start()
        sum_middle("b", c, *b_args(c))

    def activate(c):
        s = c % SLOTS
        finish((a_y(c),))
        value, slope = gelu_pair(ya_own[s, 0] + ya_in[s, 0].astype(F32))
        ha[0, c, x0, y0] = value.astype(BF16)
        ha[1, c, x0, y0] = ((ya_own[s, 1] + ya_in[s, 1].astype(F32)) * slope).astype(BF16)
        ga_y(c).start()
        totals = sum_last("b", c, *b_args(c))
        value, slope = gelu_pair(totals[0])
        hb[0, c, y0, x0] = value.astype(BF16)
        hb[1, c, y0, x0] = (totals[1] * slope).astype(BF16)
        start(gb_first(c))

    def gather_one(c):
        finish((ga_y(c),))
        start(ga_first(c))
        finish(gb_first(c))
        start(gb_second(c))

    def gather_two(c):
        finish(ga_first(c))
        start(ga_second(c))
        finish(gb_second(c))
        start((gb_y(c),))

    def multiply_out(c):
        finish(ga_second(c))
        finish((gb_y(c),))
        s = c % SLOTS
        for t in range(2):
            left_a = ha[t, c].reshape(-1, ha.shape[-1])
            left_b = hb[t, c].reshape(-1, hb.shape[-1])
            if t == 0:
                both = contract(left_a, w_ref[:WIDE], ((1,), (0,)))
                both += contract(left_b, w_ref[WIDE:], ((1,), (0,)))
            else:
                both = contract(left_a, u_ref[:, :WIDE], ((1,), (1,)))
                both += contract(left_b, u_ref[:, WIDE:], ((1,), (1,)))
            part[s, t] = both.astype(BF16).reshape(part.shape[2:])
        o_core(c).start()
        for cols, src in ((slice(None, WIDE), ha), (slice(WIDE, None), hb)):
            acc_u[:, cols] += contract(wide(c, 0), src[1, c].reshape(-1, src.shape[-1]), ((0,), (0,)))
            acc_w[cols] += contract(src[0, c].reshape(-1, src.shape[-1]), wide(c, 1), ((0,), (0,)))

    def total_one(c):
        finish((o_core(c),))
        s = c % SLOTS
        cr[c] = (cr[c].astype(F32) + part[s, :, c0].astype(F32)).astype(BF16)
        piece, transit, direct, _, mine, to = o_args(c)
        for t, way in ways:
            start(sum_first("o", c, t, way, piece, transit, direct, mine, to))

    def total_two(c):
        sum_middle("o", c, *o_args(c))

    def total_three(c):
        s = c % SLOTS
        totals = sum_last("o", c, *o_args(c))
        for t in range(2):
            first, second = totals[t][0], totals[t][1]
            yo_own[s, t] = jnp.where(h0 == 0, first, second)
            yo_out[s, t] = jnp.where(h0 == 0, second, first).astype(BF16)
        o_y(c).start()

    def total_four(c):
        s = c % SLOTS
        finish((o_y(c),))
        at = pl.ds(pl.multiple_of(c * rows, rows), rows)
        out_ref[at, :] = (yo_own[s, 0] + yo_in[c, 0].astype(F32)).astype(BF16)
        ing_ref[at, :] = (yo_own[s, 1] + yo_in[c, 1].astype(F32)).astype(BF16)

    stages = (
        gather_tokens_first, gather_tokens_second, gather_tokens_core, multiply_in,
        sum_one, sum_two, activate, gather_one, gather_two, multiply_out,
        total_one, total_two, total_three, total_four,
    )

    for c in range(CHUNKS):
        tok_y(c).start()

    def step(number, carry):
        for behind, stage in reversed(tuple(enumerate(stages))):
            @pl.when((number >= behind) & (number < behind + CHUNKS))
            def _():
                stage(number - behind)
        return carry

    lax.fori_loop(0, CHUNKS + len(stages) - 1, step, 0)
    du_ref[...] = acc_u[...].astype(BF16)
    dw_ref[...] = acc_w[...].astype(BF16)


def per_device(inputs, up_weight, down_weight, out_grad):
    tokens, width = inputs.shape
    hidden = up_weight.shape[1]
    rows = tokens // CHUNKS
    owned = rows * 2
    narrow = hidden - WIDE

    def vmem(*shape, dtype=BF16):
        return pltpu.VMEM(shape, dtype)

    scratch = [
        vmem(2, CHUNKS, 2, 4, 2, rows, width),
        vmem(SLOTS, 2, 4, 2, owned, WIDE),
        vmem(SLOTS, 2, 2, 4, owned, narrow),
        *[vmem(SLOTS, 2, 2, owned, WIDE)] * 3,
        vmem(SLOTS, 2, owned, WIDE),
        vmem(SLOTS, 2, owned, WIDE),
        vmem(SLOTS, 2, owned, WIDE, dtype=F32),
        vmem(SLOTS, 2, 4, owned, narrow),
        *[vmem(SLOTS, 2, owned, narrow)] * 3,
        vmem(2, CHUNKS, 4, 2, owned, WIDE),
        vmem(2, CHUNKS, 2, 4, owned, narrow),
        vmem(SLOTS, 2, 2, 4, 2, rows, width),
        vmem(CHUNKS, 2, 4, 2, rows, width),
        *[vmem(CHUNKS, 2, 2, rows, width)] * 3,
        vmem(SLOTS, 2, rows, width),
        vmem(CHUNKS, 2, rows, width),
        vmem(SLOTS, 2, rows, width, dtype=F32),
        vmem(width, hidden, dtype=F32),
        vmem(hidden, width, dtype=F32),
        pltpu.SemaphoreType.DMA((len(NAMES), CHUNKS)),
        pltpu.SemaphoreType.DMA((len(NAMES), CHUNKS)),
    ]
    return pl.pallas_call(
        kernel,
        out_shape=(
            jax.ShapeDtypeStruct(inputs.shape, BF16),
            jax.ShapeDtypeStruct(inputs.shape, BF16),
            jax.ShapeDtypeStruct(up_weight.shape, BF16),
            jax.ShapeDtypeStruct(down_weight.shape, BF16),
        ),
        in_specs=[pl.BlockSpec(memory_space=pltpu.VMEM)] * 4,
        out_specs=[pl.BlockSpec(memory_space=pltpu.VMEM)] * 4,
        scratch_shapes=scratch,
        compiler_params=pltpu.CompilerParams(
            collective_id=0, has_side_effects=True, vmem_limit_bytes=62 * 1024 * 1024
        ),
    )(inputs, up_weight, down_weight, out_grad)


def solution(mesh):
    placed = (
        P(("ia", "ka"), "ja"),
        P("ja", ("ka", "ia")),
        P(("ka", "ia"), "ja"),
        P(("ia", "ka"), "ja"),
    )
    return jax.shard_map(
        per_device,
        mesh=mesh,
        in_specs=placed,
        out_specs=(
            P(("ia", "ka"), "ja"),
            P(("ia", "ka"), "ja"),
            P("ja", ("ka", "ia")),
            P(("ka", "ia"), "ja"),
        ),
        check_vma=False,
    )
```

time: 951 us -> 233 us (0.25)
  waiting for transfers between devices: 831 us -> 0 us
  Pallas kernels: 0 us -> 223 us
  matrix products: 70.2 us -> 0 us
  local copies, waits for them, and re-layouts: 26 us -> 8.01 us
  between operations: 14.4 us -> 0.64 us
    reduce_scatter x10 -> x0, waiting for transfers between devices: 424 us -> none  [the longest x4 168 us: forward(): lax.psum_scatter(grad.astype(jnp.bfloat16), 'ja', scatter_dimension=0, ti...]
    all_gather x10 -> x0, waiting for transfers between devices: 403 us -> none  [the longest x4 154 us: forward(): lax.all_gather(preact_grad, 'ja', axis=0, tiled=True)]
    pallas_call x0 -> x1, Pallas kernels: none -> 223 us  [per_device(): pl.pallas_call(kernel, out_shape=(jax.ShapeDtypeStruct(inputs.shape, BF16...]
    dot_general x12 -> x0, matrix products: 70.2 us -> none  [the longest x5 27.5 us: contract_cols(): lax.dot_general(left, right, (((1,), (1,)), ((), ())), preferred_element_...]
    unnamed x11 -> x6, local copies, waits for them, and re-layouts: 20.4 us -> 8.01 us
  transfers between devices with their start and end apart: 20 -> 0, of which waited for: 20 -> 0; matrix products, arithmetic and copies ran while one was open for 11% -> 0% of each run, Pallas kernels for 0% -> 0%
where the time goes in v2:
time: 233 us; the launch traced here: 232 us
  Pallas kernels  223 us (96%)
  local copies, waits for them, and re-layouts  8.01 us (3%)
    pallas_call x1, Pallas kernels, per_device(): pl.pallas_call(kernel, out_shape=(jax.ShapeDtypeStruct(inputs.shape, BF16...  223 us
    unnamed x6, local copies, waits for them, and re-layouts  8.01 us

profile of v2, /device:TPU:0, one launch (start us, length us, event | category | flops | bytes accessed | tf_op | source)
XLA Modules:
  0.0 231.6 jit_solution(11126386209333475561)
XLA Ops:
  0.6 223.0 %shard_map.75 = (bf16[128,768]{1,0:T(8,128)(2,1)}, bf16[128,768]{1,0:T(8,128)(2,1)}, bf16[768,1536]{1,0:T(8,128)(2,1)}, bf16[1536,768]{1,0:T(8,128)(2,1)}) custom-call(bf16[128,768]{1,0:T(8,128)(2,1)} %x_ref.1, bf16[768,1536]{1,0:T(8,128)(2,1)} %u_ref.1, bf16[1536,768]{1,0:T(8,128)(2,1)} %w_ref.1, bf16[128,768]{1,0:T(8,128)(2,1)} %g_ref.1), custom_call_target="tpu_custom_call" | custom-call | tf_op jit(solution)/shard_map/pallas_call | solution.py:389
  223.6 1.6 copy.12
  225.2 1.6 copy.13
  226.8 0.0 copy-start
  226.8 3.4 %copy.14 = bf16[768,1536]{1,0:T(8,128)(2,1)} copy(bf16[768,1536]{1,0:T(8,128)(2,1)} %get-tuple-element.10) | data formatting | bytes 4718592
  230.2 0.0 copy-done
  230.2 1.4 copy.15
Async XLA Ops:
  226.8 3.4 %copy-start = (bf16[1536,768]{1,0:T(8,128)(2,1)S(1)}, bf16[1536,768]{1,0:T(8,128)(2,1)}, u32[]{:S(2)}) copy-start(bf16[1536,768]{1,0:T(8,128)(2,1)} %get-tuple-element.11) | copy-start | bytes 7077892

commit v3 on v2

--- a/solution.py
+++ b/solution.py
@@ -16,7 +16,7 @@
 
 CHUNKS = 8
 SLOTS = 4
-WIDE = 1024
+WIDE = 896
 
 NAMES = (
     "tok_y", "tok_z_up", "tok_z_down", "tok_z0", "tok_z1", "tok_core",
@@ -42,7 +42,8 @@
 
 
 def kernel(
-    x_ref, u_ref, w_ref, g_ref, out_ref, ing_ref, du_ref, dw_ref,
+    x_ref, u_hbm, w_hbm, g_ref, out_ref, ing_ref, du_hbm, dw_hbm,
+    u_ref, w_ref, du_ref, dw_ref, local_sem,
     tok, pa, pb, ta, da, sa, ya_out, ya_in, ya_own, rb, tb, db, sb, ha, hb,
     part, cr, tz, dz, sz, yo_out, yo_in, yo_own, acc_u, acc_w, send_sem, recv_sem,
 ):
@@ -64,14 +65,19 @@
     c_pair = (z0, ja, h0 * 2 + 1 - c0)
     ways = ((0, 1), (1, -1))
 
+    load_u = pltpu.make_async_copy(u_hbm, u_ref, local_sem.at[0])
+    load_w = pltpu.make_async_copy(w_hbm, w_ref, local_sem.at[1])
+    store_u = pltpu.make_async_copy(du_ref, du_hbm, local_sem.at[2])
+    store_w = pltpu.make_async_copy(dw_ref, dw_hbm, local_sem.at[3])
+    load_u.start()
+    load_w.start()
+
     barrier = pltpu.get_barrier_semaphore()
     for other in (at_x(1), at_x(-1), at_z(1), at_z(-1), y_pair, h_pair, c_pair):
         pl.semaphore_signal(barrier, inc=1, device_id=other, device_id_type=MESH)
     for c in range(CHUNKS):
         tok[0, c, c0, z0, h0] = x_ref[c * rows:(c + 1) * rows]
         tok[1, c, c0, z0, h0] = g_ref[c * rows:(c + 1) * rows]
-    acc_u[...] = jnp.zeros_like(acc_u)
-    acc_w[...] = jnp.zeros_like(acc_w)
     pl.semaphore_wait(barrier, 7)
 
     def copy(name, c, src, dst, to):
@@ -301,6 +307,8 @@
                 both += contract(left_b, u_ref[:, WIDE:], ((1,), (1,)))
             part[s, t] = both.astype(BF16).reshape(part.shape[2:])
         o_core(c).start()
+
+    def add_grads(c):
         for cols, src in ((slice(None, WIDE), ha), (slice(WIDE, None), hb)):
             acc_u[:, cols] += contract(wide(c, 0), src[1, c].reshape(-1, src.shape[-1]), ((0,), (0,)))
             acc_w[cols] += contract(src[0, c].reshape(-1, src.shape[-1]), wide(c, 1), ((0,), (0,)))
@@ -312,9 +320,17 @@
         piece, transit, direct, _, mine, to = o_args(c)
         for t, way in ways:
             start(sum_first("o", c, t, way, piece, transit, direct, mine, to))
+        add_grads(c)
 
     def total_two(c):
         sum_middle("o", c, *o_args(c))
+
+        @pl.when(c == CHUNKS - 1)
+        def _():
+            du_ref[...] = acc_u[...].astype(BF16)
+            store_u.start()
+            dw_ref[...] = acc_w[...].astype(BF16)
+            store_w.start()
 
     def total_three(c):
         s = c % SLOTS
@@ -340,6 +356,10 @@
 
     for c in range(CHUNKS):
         tok_y(c).start()
+    acc_u[...] = jnp.zeros_like(acc_u)
+    acc_w[...] = jnp.zeros_like(acc_w)
+    load_u.wait()
+    load_w.wait()
 
     def step(number, carry):
         for behind, stage in reversed(tuple(enumerate(stages))):
@@ -349,8 +369,30 @@
         return carry
 
     lax.fori_loop(0, CHUNKS + len(stages) - 1, step, 0)
-    du_ref[...] = acc_u[...].astype(BF16)
-    dw_ref[...] = acc_w[...].astype(BF16)
+    store_u.wait()
+    store_w.wait()
+
+
+def hand_on(*refs):
+    sources, targets, held, sem = refs[:4], refs[4:8], refs[8:12], refs[12]
+    copies = []
+    for source, target, room in zip(sources, targets, held):
+        parts = max(1, source.shape[0] // 384)
+        rows = source.shape[0] // parts
+        for number in range(parts):
+            at = pl.ds(number * rows, rows)
+            place = len(copies)
+            copies.append((
+                pltpu.make_async_copy(source.at[at], room.at[at], sem.at[0, place]),
+                pltpu.make_async_copy(room.at[at], target.at[at], sem.at[1, place]),
+            ))
+    for load, _ in copies:
+        load.start()
+    for load, store in copies:
+        load.wait()
+        store.start()
+    for _, store in copies:
+        store.wait()
 
 
 def per_device(inputs, up_weight, down_weight, out_grad):
@@ -364,6 +406,11 @@
         return pltpu.VMEM(shape, dtype)
 
     scratch = [
+        vmem(width, hidden),
+        vmem(hidden, width),
+        vmem(width, hidden),
+        vmem(hidden, width),
+        pltpu.SemaphoreType.DMA((4,)),
         vmem(2, CHUNKS, 2, 4, 2, rows, width),
         vmem(SLOTS, 2, 4, 2, owned, WIDE),
         vmem(SLOTS, 2, 2, 4, owned, narrow),
@@ -386,21 +433,31 @@
         pltpu.SemaphoreType.DMA((len(NAMES), CHUNKS)),
         pltpu.SemaphoreType.DMA((len(NAMES), CHUNKS)),
     ]
-    return pl.pallas_call(
+    results = (
+        jax.ShapeDtypeStruct(inputs.shape, BF16),
+        jax.ShapeDtypeStruct(inputs.shape, BF16),
+        jax.ShapeDtypeStruct(up_weight.shape, BF16),
+        jax.ShapeDtypeStruct(down_weight.shape, BF16),
+    )
+    near, far = pl.BlockSpec(memory_space=pltpu.VMEM), pl.BlockSpec(memory_space=pl.ANY)
+    made = pl.pallas_call(
         kernel,
-        out_shape=(
-            jax.ShapeDtypeStruct(inputs.shape, BF16),
-            jax.ShapeDtypeStruct(inputs.shape, BF16),
-            jax.ShapeDtypeStruct(up_weight.shape, BF16),
-            jax.ShapeDtypeStruct(down_weight.shape, BF16),
-        ),
-        in_specs=[pl.BlockSpec(memory_space=pltpu.VMEM)] * 4,
-        out_specs=[pl.BlockSpec(memory_space=pltpu.VMEM)] * 4,
+        out_shape=results,
+        in_specs=[near, far, far, near],
+        out_specs=[near, near, far, far],
         scratch_shapes=scratch,
         compiler_params=pltpu.CompilerParams(
             collective_id=0, has_side_effects=True, vmem_limit_bytes=62 * 1024 * 1024
         ),
     )(inputs, up_weight, down_weight, out_grad)
+    return pl.pallas_call(
+        hand_on,
+        out_shape=results,
+        in_specs=[far] * 4,
+        out_specs=[far] * 4,
+        scratch_shapes=[vmem(*one.shape) for one in results] + [pltpu.SemaphoreType.DMA((2, 8))],
+        compiler_params=pltpu.CompilerParams(vmem_limit_bytes=62 * 1024 * 1024),
+    )(*made)
 
 
 def solution(mesh):

time: 233 us -> 218 us (0.936)
  local copies, waits for them, and re-layouts: 8.01 us -> 0 us
  Pallas kernels: 223 us -> 217 us
    unnamed x6 -> x0, local copies, waits for them, and re-layouts: 8.01 us -> none
    pallas_call x1 -> x2, Pallas kernels: 223 us -> 217 us  [the longest x1 213 us: per_device(): pl.pallas_call(kernel, out_shape=results, in_specs=[near, far, far, near]...]
where the time goes in v3:
time: 218 us
  Pallas kernels  217 us (100%)
    pallas_call x1, Pallas kernels, per_device(): pl.pallas_call(kernel, out_shape=results, in_specs=[near, far, far, near]...  213 us

profile of v3, /device:TPU:0, one launch (start us, length us, event | category | flops | bytes accessed | tf_op | source)
XLA Modules:
  0.0 217.8 jit_solution(16948119708017676127)
XLA Ops:
  0.6 212.9 %shard_map.75 = (bf16[128,768]{1,0:T(8,128)(2,1)}, bf16[128,768]{1,0:T(8,128)(2,1)}, bf16[768,1536]{1,0:T(8,128)(2,1)}, bf16[1536,768]{1,0:T(8,128)(2,1)}) custom-call(bf16[128,768]{1,0:T(8,128)(2,1)} %x_ref.1, bf16[768,1536]{1,0:T(8,128)(2,1)} %u_hbm.1, bf16[1536,768]{1,0:T(8,128)(2,1)} %w_hbm.1, bf16[128,768]{1,0:T(8,128)(2,1)} %g_ref.1), custom_call_target="tpu_custom_call" | custom-call | tf_op jit(solution)/shard_map/pallas_call | solution.py:443
  213.5 4.2 %shard_map.76 = (bf16[128,768]{1,0:T(8,128)(2,1)}, bf16[128,768]{1,0:T(8,128)(2,1)}, bf16[768,1536]{1,0:T(8,128)(2,1)}, bf16[1536,768]{1,0:T(8,128)(2,1)}) custom-call(bf16[128,768]{1,0:T(8,128)(2,1)} %get-tuple-element.8.refs_0_, bf16[128,768]{1,0:T(8,128)(2,1)} %get-tuple-element.9.refs_1_, bf16[768,1536]{1,0:T(8,128)(2,1)} %get-tuple-element.10.refs_2_, ...), custom_call_target="tpu_custom_call" | custom-call | tf_op jit(solution)/shard_map/pallas_call | solution.py:453

commit v4 on v3

--- a/solution.py
+++ b/solution.py
@@ -16,16 +16,20 @@
 
 CHUNKS = 8
 SLOTS = 4
+HELD = 3
 WIDE = 896
 
+RECEIVED = 3
+SENT = 2
 NAMES = (
-    "tok_y", "tok_z_up", "tok_z_down", "tok_z0", "tok_z1", "tok_core",
+    "tok_z1", "tok_z2", "tok_z3", "tok_core",
     "a_t0", "a_t1", "a_d0", "a_d1", "a_s0", "a_s1", "a_y",
-    "b_t0", "b_t1", "b_d0", "b_d1", "b_s0", "b_s1", "b_y",
-    "ga_y", "ga_up", "ga_down", "ga_x0", "ga_x1",
-    "gb_y", "gb_up", "gb_down", "gb_x0", "gb_x1",
-    "o_core", "o_t0", "o_t1", "o_d0", "o_d1", "o_s0", "o_s1", "o_y",
+    "b_t0", "b_t1", "b_d0", "b_d1", "b_s0", "b_s1", "b_y0", "b_y1",
+    "ga_y", "ga_up", "ga_down", "ga_x0", "ga_x1", "gp_up", "gp_down", "gp_x0", "gp_x1",
+    "gb_y0", "gb_y1", "gb_y2", "gb_y3", "gb_up", "gb_down", "gb_x0", "gb_x1",
+    "o_core0", "o_core1", "o_z1", "o_z2", "o_z3", "o_y",
 )
+PEERS = tuple((step, turn) for step in range(4) for turn in range(2))[1:]
 INDEX = {name: place for place, name in enumerate(NAMES)}
 
 
@@ -42,17 +46,18 @@
 
 
 def kernel(
-    x_ref, u_hbm, w_hbm, g_ref, out_ref, ing_ref, du_hbm, dw_hbm,
+    x_hbm, u_hbm, w_hbm, g_hbm, out_ref, ing_ref, du_hbm, dw_hbm,
     u_ref, w_ref, du_ref, dw_ref, local_sem,
     tok, pa, pb, ta, da, sa, ya_out, ya_in, ya_own, rb, tb, db, sb, ha, hb,
-    part, cr, tz, dz, sz, yo_out, yo_in, yo_own, acc_u, acc_w, send_sem, recv_sem,
+    part, cr, zr, last_in, yo_out, yo_in, yo_own, acc_u, acc_w, send_sem, recv_sem, peer_sem, tok_sem,
 ):
     z0 = lax.axis_index("ia")
     ja = lax.axis_index("ja")
     ka = lax.axis_index("ka")
     y0, x0 = ja // 4, ja % 4
     h0, c0 = ka // 2, ka % 2
-    rows = x_ref.shape[0] // CHUNKS
+    rows = x_hbm.shape[1]
+    last = CHUNKS - 1
 
     def at_x(step):
         return (z0, y0 * 4 + (x0 + step + 4) % 4, ka)
@@ -65,25 +70,26 @@
     c_pair = (z0, ja, h0 * 2 + 1 - c0)
     ways = ((0, 1), (1, -1))
 
+    barrier = pltpu.get_barrier_semaphore()
+    peers = [((z0 + step) % 4, ja, (h0 + turn) % 2 * 2 + c0) for step, turn in PEERS]
+    for other in [at_x(1), at_x(-1), y_pair, c_pair] + peers:
+        pl.semaphore_signal(barrier, inc=1, device_id=other, device_id_type=MESH)
+    load_x = pltpu.make_async_copy(x_hbm, tok.at[0, :, c0, z0, h0], local_sem.at[4])
+    load_g = pltpu.make_async_copy(g_hbm, tok.at[1, :, c0, z0, h0], local_sem.at[5])
     load_u = pltpu.make_async_copy(u_hbm, u_ref, local_sem.at[0])
     load_w = pltpu.make_async_copy(w_hbm, w_ref, local_sem.at[1])
     store_u = pltpu.make_async_copy(du_ref, du_hbm, local_sem.at[2])
     store_w = pltpu.make_async_copy(dw_ref, dw_hbm, local_sem.at[3])
-    load_u.start()
-    load_w.start()
-
-    barrier = pltpu.get_barrier_semaphore()
-    for other in (at_x(1), at_x(-1), at_z(1), at_z(-1), y_pair, h_pair, c_pair):
-        pl.semaphore_signal(barrier, inc=1, device_id=other, device_id_type=MESH)
-    for c in range(CHUNKS):
-        tok[0, c, c0, z0, h0] = x_ref[c * rows:(c + 1) * rows]
-        tok[1, c, c0, z0, h0] = g_ref[c * rows:(c + 1) * rows]
-    pl.semaphore_wait(barrier, 7)
+    for one in (load_x, load_g, load_u, load_w):
+        one.start()
+    load_x.wait()
+    load_g.wait()
+    pl.semaphore_wait(barrier, 4 + len(PEERS))
 
     def copy(name, c, src, dst, to):
         return pltpu.make_async_remote_copy(
             src_ref=src, dst_ref=dst,
-            send_sem=send_sem.at[INDEX[name], c], recv_sem=recv_sem.at[INDEX[name], c],
+            send_sem=send_sem.at[INDEX[name], c % SENT], recv_sem=recv_sem.at[INDEX[name], c % RECEIVED],
             device_id=to, device_id_type=MESH,
         )
 
@@ -138,20 +144,38 @@
 
     def tok_y(c):
         here = tok.at[:, c, c0, z0, h0]
-        return copy("tok_y", c, here, here, h_pair)
-
-    def tok_z(c, z):
-        return tok.at[:, c, c0, z]
-
-    def tok_z_one(c, t, z):
-        return tok.at[t, c, c0, z]
+        return pltpu.make_async_remote_copy(
+            src_ref=here, dst_ref=here, send_sem=tok_sem.at[0, c], recv_sem=tok_sem.at[1, c],
+            device_id=h_pair, device_id_type=MESH,
+        )
+
+    def tok_z(c):
+        here = tok.at[:, c, c0, z0]
+        return [copy(f"tok_z{step}", c, here, here, at_z(step)) for step in (1, 2, 3)]
+
+    def peer_copy(which, place, src, dst):
+        return pltpu.make_async_remote_copy(
+            src_ref=src, dst_ref=dst,
+            send_sem=peer_sem.at[which, 0, place], recv_sem=peer_sem.at[which, 1, place],
+            device_id=peers[place], device_id_type=MESH,
+        )
+
+    def first_tokens():
+        here = tok.at[:, 0, c0, z0, h0]
+        return [peer_copy(0, place, here, here) for place in range(len(PEERS))]
+
+    def last_sums():
+        return [
+            peer_copy(1, place, cr.at[last, :, (z0 + step) % 4, (h0 + turn) % 2], last_in.at[place])
+            for place, (step, turn) in enumerate(PEERS)
+        ]
 
     def tok_core(c):
         here = tok.at[:, c, c0]
         return copy("tok_core", c, here, here, c_pair)
 
     def a_piece(c, t, x):
-        return pa.at[c % SLOTS, t, x]
+        return pa.at[c % HELD, t, x]
 
     def a_args(c):
         s = c % SLOTS
@@ -161,9 +185,9 @@
         s = c % SLOTS
         return copy("a_y", c, ya_out.at[s], ya_in.at[s], y_pair)
 
-    def b_y(c):
-        s = c % SLOTS
-        return copy("b_y", c, pb.at[s, :, 1 - y0], rb.at[s], y_pair)
+    def b_y(c, t):
+        s = c % SLOTS
+        return copy(f"b_y{t}", c, pb.at[c % HELD, t, 1 - y0], rb.at[s, t], y_pair)
 
     def b_piece(c, t, x):
         return rb.at[c % SLOTS, t, x]
@@ -176,15 +200,21 @@
         here = ha.at[:, c, x0, y0]
         return copy("ga_y", c, here, here, y_pair)
 
-    def gb_y(c):
-        here = hb.at[:, c, y0]
-        return copy("gb_y", c, here, here, y_pair)
+    def gb_y(c, step):
+        here = hb.at[:, c, y0, (x0 + step) % 4]
+        return copy(f"gb_y{step}", c, here, here, y_pair)
 
     def ga_first(c):
-        return gather_first("ga", c, lambda x: ha.at[:, c, x], x0, at_x)
+        return gather_first("ga", c, lambda x: ha.at[:, c, x, y0], x0, at_x)
 
     def ga_second(c):
-        return gather_second("ga", c, lambda t, x: ha.at[t, c, x], x0, at_x, "x")
+        return gather_second("ga", c, lambda t, x: ha.at[t, c, x, y0], x0, at_x, "x")
+
+    def gp_first(c):
+        return gather_first("gp", c, lambda x: ha.at[:, c, x, 1 - y0], x0, at_x)
+
+    def gp_second(c):
+        return gather_second("gp", c, lambda t, x: ha.at[t, c, x, 1 - y0], x0, at_x, "x")
 
     def gb_first(c):
         return gather_first("gb", c, lambda x: hb.at[:, c, y0, x], x0, at_x)
@@ -192,17 +222,14 @@
     def gb_second(c):
         return gather_second("gb", c, lambda t, x: hb.at[t, c, y0, x], x0, at_x, "x")
 
-    def tok_first(c):
-        return gather_first("tok_z", c, functools.partial(tok_z, c), z0, at_z)
-
-    def tok_second(c):
-        return gather_second("tok", c, functools.partial(tok_z_one, c), z0, at_z, "z")
-
-    def o_core(c):
-        return copy("o_core", c, part.at[c % SLOTS, :, 1 - c0], cr.at[c], c_pair)
-
-    def o_args(c):
-        return (lambda t, z: cr.at[c, t, z]), tz.at[c], dz.at[c], sz.at[c], z0, at_z
+    def o_core(c, t):
+        return copy(f"o_core{t}", c, part.at[c % HELD, t, 1 - c0], cr.at[c, t], c_pair)
+
+    def o_z(c):
+        return [
+            copy(f"o_z{step}", c, cr.at[c, :, (z0 + step) % 4], zr.at[c, step - 1], at_z(step))
+            for step in (1, 2, 3)
+        ]
 
     def o_y(c):
         return copy("o_y", c, yo_out.at[c % SLOTS], yo_in.at[c], h_pair)
@@ -220,21 +247,24 @@
     def wide(c, t):
         return tok[t, c].reshape(-1, tok.shape[-1])
 
-    def gather_tokens_first(c):
+    def gather_tokens(c):
         finish((tok_y(c),))
-        start(tok_first(c))
-
-    def gather_tokens_second(c):
-        finish(tok_first(c))
-        start(tok_second(c))
+        start(tok_z(c))
 
     def gather_tokens_core(c):
-        finish(tok_second(c))
+        @pl.when(c > 0)
+        def _():
+            finish(tok_z(c))
+
+        @pl.when(c == 0)
+        def _():
+            finish(first_tokens())
+
         start((tok_core(c),))
 
     def multiply_in(c):
         finish((tok_core(c),))
-        s = c % SLOTS
+        s = c % HELD
         for t, way in ways:
             if t == 0:
                 both = contract(wide(c, 0), u_ref[...], ((1,), (0,)))
@@ -244,18 +274,19 @@
             pa[s, t] = both[:, :WIDE].reshape(pa.shape[2:])
             pb[s, t] = both[:, WIDE:].reshape(pb.shape[2:])
             piece, transit, direct, _, mine, to = a_args(c)
+            b_y(c, t).start()
             start(sum_first("a", c, t, way, piece, transit, direct, mine, to))
-        b_y(c).start()
 
     def sum_one(c):
         sum_middle("a", c, *a_args(c))
-        b_y(c).wait_recv()
-        s = c % SLOTS
-        rb[s] = (rb[s].astype(F32) + pb[s, :, y0].astype(F32)).astype(BF16)
+        s = c % SLOTS
         piece, transit, direct, _, mine, to = b_args(c)
         for t, way in ways:
+            b_y(c, t).wait_recv()
+            rb[s, t] = (rb[s, t].astype(F32) + pb[c % HELD, t, y0].astype(F32)).astype(BF16)
             start(sum_first("b", c, t, way, piece, transit, direct, mine, to))
-        b_y(c).wait_send()
+        for t in range(2):
+            b_y(c, t).wait_send()
 
     def sum_two(c):
         s = c % SLOTS
@@ -274,28 +305,36 @@
         ha[0, c, x0, y0] = value.astype(BF16)
         ha[1, c, x0, y0] = ((ya_own[s, 1] + ya_in[s, 1].astype(F32)) * slope).astype(BF16)
         ga_y(c).start()
+        start(ga_first(c))
         totals = sum_last("b", c, *b_args(c))
         value, slope = gelu_pair(totals[0])
         hb[0, c, y0, x0] = value.astype(BF16)
         hb[1, c, y0, x0] = (totals[1] * slope).astype(BF16)
+        gb_y(c, 0).start()
         start(gb_first(c))
 
     def gather_one(c):
         finish((ga_y(c),))
-        start(ga_first(c))
+        start(gp_first(c))
         finish(gb_first(c))
         start(gb_second(c))
-
-    def gather_two(c):
+        start((gb_y(c, 1), gb_y(c, 3)))
+        finish((gb_y(c, 0),))
         finish(ga_first(c))
         start(ga_second(c))
+
+    def gather_two(c):
+        finish(gp_first(c))
+        start(gp_second(c))
         finish(gb_second(c))
-        start((gb_y(c),))
+        gb_y(c, 2).start()
+        finish((gb_y(c, 1), gb_y(c, 3)))
 
     def multiply_out(c):
         finish(ga_second(c))
-        finish((gb_y(c),))
-        s = c % SLOTS
+        finish(gp_second(c))
+        finish((gb_y(c, 2),))
+        s = c % HELD
         for t in range(2):
             left_a = ha[t, c].reshape(-1, ha.shape[-1])
             left_b = hb[t, c].reshape(-1, hb.shape[-1])
@@ -306,7 +345,7 @@
                 both = contract(left_a, u_ref[:, :WIDE], ((1,), (1,)))
                 both += contract(left_b, u_ref[:, WIDE:], ((1,), (1,)))
             part[s, t] = both.astype(BF16).reshape(part.shape[2:])
-        o_core(c).start()
+            o_core(c, t).start()
 
     def add_grads(c):
         for cols, src in ((slice(None, WIDE), ha), (slice(WIDE, None), hb)):
@@ -314,47 +353,66 @@
             acc_w[cols] += contract(src[0, c].reshape(-1, src.shape[-1]), wide(c, 1), ((0,), (0,)))
 
     def total_one(c):
-        finish((o_core(c),))
-        s = c % SLOTS
-        cr[c] = (cr[c].astype(F32) + part[s, :, c0].astype(F32)).astype(BF16)
-        piece, transit, direct, _, mine, to = o_args(c)
-        for t, way in ways:
-            start(sum_first("o", c, t, way, piece, transit, direct, mine, to))
-        add_grads(c)
+        s = c % HELD
+        for t in range(2):
+            finish((o_core(c, t),))
+            cr[c, t] = (cr[c, t].astype(F32) + part[s, t, c0].astype(F32)).astype(BF16)
+
+        @pl.when(c < last)
+        def _():
+            start(o_z(c))
+
+        @pl.when(c == last)
+        def _():
+            start(last_sums())
 
     def total_two(c):
-        sum_middle("o", c, *o_args(c))
-
-        @pl.when(c == CHUNKS - 1)
+        s = c % SLOTS
+
+        @pl.when(c < last)
+        def _():
+            finish(o_z(c))
+            for t in range(2):
+                first, second = (
+                    cr[c, t, z0, h].astype(F32) + zr[c, 0, t, h].astype(F32)
+                    + zr[c, 1, t, h].astype(F32) + zr[c, 2, t, h].astype(F32)
+                    for h in range(2)
+                )
+                yo_own[s, t] = jnp.where(h0 == 0, first, second)
+                yo_out[s, t] = jnp.where(h0 == 0, second, first).astype(BF16)
+            o_y(c).start()
+
+        @pl.when(c == last)
         def _():
             du_ref[...] = acc_u[...].astype(BF16)
             store_u.start()
             dw_ref[...] = acc_w[...].astype(BF16)
             store_w.start()
+            finish(last_sums())
+            for t, ref in enumerate((out_ref, ing_ref)):
+                total = cr[c, t, z0, h0].astype(F32)
+                for place in range(len(PEERS)):
+                    total += last_in[place, t].astype(F32)
+                ref[last * rows:, :] = total.astype(BF16)
 
     def total_three(c):
         s = c % SLOTS
-        totals = sum_last("o", c, *o_args(c))
-        for t in range(2):
-            first, second = totals[t][0], totals[t][1]
-            yo_own[s, t] = jnp.where(h0 == 0, first, second)
-            yo_out[s, t] = jnp.where(h0 == 0, second, first).astype(BF16)
-        o_y(c).start()
-
-    def total_four(c):
-        s = c % SLOTS
-        finish((o_y(c),))
-        at = pl.ds(pl.multiple_of(c * rows, rows), rows)
-        out_ref[at, :] = (yo_own[s, 0] + yo_in[c, 0].astype(F32)).astype(BF16)
-        ing_ref[at, :] = (yo_own[s, 1] + yo_in[c, 1].astype(F32)).astype(BF16)
+
+        @pl.when(c < last)
+        def _():
+            finish((o_y(c),))
+            at = pl.ds(pl.multiple_of(c * rows, rows), rows)
+            out_ref[at, :] = (yo_own[s, 0] + yo_in[c, 0].astype(F32)).astype(BF16)
+            ing_ref[at, :] = (yo_own[s, 1] + yo_in[c, 1].astype(F32)).astype(BF16)
 
     stages = (
-        gather_tokens_first, gather_tokens_second, gather_tokens_core, multiply_in,
-        sum_one, sum_two, activate, gather_one, gather_two, multiply_out,
-        total_one, total_two, total_three, total_four,
+        (10, total_three), (9, total_two), (8, total_one), (7, multiply_out), (6, gather_two),
+        (5, gather_one), (4, activate), (3, sum_two), (2, sum_one), (1, multiply_in),
+        (0, gather_tokens_core), (-1, gather_tokens), (8, add_grads),
     )
 
-    for c in range(CHUNKS):
+    start(first_tokens())
+    for c in range(1, CHUNKS):
         tok_y(c).start()
     acc_u[...] = jnp.zeros_like(acc_u)
     acc_w[...] = jnp.zeros_like(acc_w)
@@ -362,13 +420,13 @@
     load_w.wait()
 
     def step(number, carry):
-        for behind, stage in reversed(tuple(enumerate(stages))):
+        for behind, stage in stages:
             @pl.when((number >= behind) & (number < behind + CHUNKS))
             def _():
                 stage(number - behind)
         return carry
 
-    lax.fori_loop(0, CHUNKS + len(stages) - 1, step, 0)
+    lax.fori_loop(0, CHUNKS + 9, step, 0)
     store_u.wait()
     store_w.wait()
 
@@ -410,10 +468,10 @@
         vmem(hidden, width),
         vmem(width, hidden),
         vmem(hidden, width),
-        pltpu.SemaphoreType.DMA((4,)),
+        pltpu.SemaphoreType.DMA((6,)),
         vmem(2, CHUNKS, 2, 4, 2, rows, width),
-        vmem(SLOTS, 2, 4, 2, owned, WIDE),
-        vmem(SLOTS, 2, 2, 4, owned, narrow),
+        vmem(HELD, 2, 4, 2, owned, WIDE),
+        vmem(HELD, 2, 2, 4, owned, narrow),
         *[vmem(SLOTS, 2, 2, owned, WIDE)] * 3,
         vmem(SLOTS, 2, owned, WIDE),
         vmem(SLOTS, 2, owned, WIDE),
@@ -422,16 +480,19 @@
         *[vmem(SLOTS, 2, owned, narrow)] * 3,
         vmem(2, CHUNKS, 4, 2, owned, WIDE),
         vmem(2, CHUNKS, 2, 4, owned, narrow),
-        vmem(SLOTS, 2, 2, 4, 2, rows, width),
+        vmem(HELD, 2, 2, 4, 2, rows, width),
         vmem(CHUNKS, 2, 4, 2, rows, width),
-        *[vmem(CHUNKS, 2, 2, rows, width)] * 3,
+        vmem(CHUNKS, 3, 2, 2, rows, width),
+        vmem(len(PEERS), 2, rows, width),
         vmem(SLOTS, 2, rows, width),
         vmem(CHUNKS, 2, rows, width),
         vmem(SLOTS, 2, rows, width, dtype=F32),
         vmem(width, hidden, dtype=F32),
         vmem(hidden, width, dtype=F32),
-        pltpu.SemaphoreType.DMA((len(NAMES), CHUNKS)),
-        pltpu.SemaphoreType.DMA((len(NAMES), CHUNKS)),
+        pltpu.SemaphoreType.DMA((len(NAMES), SENT)),
+        pltpu.SemaphoreType.DMA((len(NAMES), RECEIVED)),
+        pltpu.SemaphoreType.DMA((2, 2, len(PEERS))),
+        pltpu.SemaphoreType.DMA((2, CHUNKS)),
     ]
     results = (
         jax.ShapeDtypeStruct(inputs.shape, BF16),
@@ -443,13 +504,16 @@
     made = pl.pallas_call(
         kernel,
         out_shape=results,
-        in_specs=[near, far, far, near],
+        in_specs=[far] * 4,
         out_specs=[near, near, far, far],
         scratch_shapes=scratch,
         compiler_params=pltpu.CompilerParams(
             collective_id=0, has_side_effects=True, vmem_limit_bytes=62 * 1024 * 1024
         ),
-    )(inputs, up_weight, down_weight, out_grad)
+    )(
+        inputs.reshape(CHUNKS, rows, width), up_weight, down_weight,
+        out_grad.reshape(CHUNKS, rows, width),
+    )
     return pl.pallas_call(
         hand_on,
         out_shape=results,

time: 218 us -> 208 us (0.954)
  Pallas kernels: 217 us -> 207 us
    pallas_call x1, Pallas kernels: 213 us -> 203 us  [per_device(): pl.pallas_call(kernel, out_shape=results, in_specs=[far] * 4, out_specs=[...]
where the time goes in v4:
time: 208 us
  Pallas kernels  207 us (100%)
    pallas_call x1, Pallas kernels, per_device(): pl.pallas_call(kernel, out_shape=results, in_specs=[far] * 4, out_specs=[...  203 us
    pallas_call x1, Pallas kernels, per_device(): pl.pallas_call(hand_on, out_shape=results, in_specs=[far] * 4, out_specs=...  4.22 us

profile of v4, /device:TPU:0, one launch (start us, length us, event | category | flops | bytes accessed | tf_op | source)
XLA Modules:
  0.0 207.7 jit_solution(5305411671646466843)
XLA Ops:
  0.6 202.8 %shard_map.75 = (bf16[128,768]{1,0:T(8,128)(2,1)}, bf16[128,768]{1,0:T(8,128)(2,1)}, bf16[768,1536]{1,0:T(8,128)(2,1)}, bf16[1536,768]{1,0:T(8,128)(2,1)}) custom-call(bf16[8,16,768]{2,1,0:T(8,128)(2,1)} %bitcast.2, bf16[768,1536]{1,0:T(8,128)(2,1)} %u_hbm.1, bf16[1536,768]{1,0:T(8,128)(2,1)} %w_hbm.1, bf16[8,16,768]{2,1,0:T(8,128)(2,1)} %bitcast.3), custom_call_target="tpu_custom_call" | custom-call | tf_op jit(solution)/shard_map/pallas_call | solution.py:504
  203.5 4.2 %shard_map.76 = (bf16[128,768]{1,0:T(8,128)(2,1)}, bf16[128,768]{1,0:T(8,128)(2,1)}, bf16[768,1536]{1,0:T(8,128)(2,1)}, bf16[1536,768]{1,0:T(8,128)(2,1)}) custom-call(bf16[128,768]{1,0:T(8,128)(2,1)} %get-tuple-element.8.refs_0_, bf16[128,768]{1,0:T(8,128)(2,1)} %get-tuple-element.9.refs_1_, bf16[768,1536]{1,0:T(8,128)(2,1)} %get-tuple-element.10.refs_2_, ...), custom_call_target="tpu_custom_call" | custom-call | tf_op jit(solution)/shard_map/pallas_call | solution.py:517

commit v5 on v4

--- a/solution.py
+++ b/solution.py
@@ -14,23 +14,32 @@
 BF16 = jnp.bfloat16
 F32 = jnp.float32
 
-CHUNKS = 8
+CHUNKS = 16
 SLOTS = 4
+PAIRED = 5
 HELD = 3
 WIDE = 896
 
 RECEIVED = 3
 SENT = 2
+EARLY = ("a_t0", "a_t1", "a_d0", "a_d1", "b_y0", "b_y1")
 NAMES = (
-    "tok_z1", "tok_z2", "tok_z3", "tok_core",
+    "tok_core0", "tok_core1",
     "a_t0", "a_t1", "a_d0", "a_d1", "a_s0", "a_s1", "a_y",
     "b_t0", "b_t1", "b_d0", "b_d1", "b_s0", "b_s1", "b_y0", "b_y1",
     "ga_y", "ga_up", "ga_down", "ga_x0", "ga_x1", "gp_up", "gp_down", "gp_x0", "gp_x1",
     "gb_y0", "gb_y1", "gb_y2", "gb_y3", "gb_up", "gb_down", "gb_x0", "gb_x1",
-    "o_core0", "o_core1", "o_z1", "o_z2", "o_z3", "o_y",
+    "o_core0", "o_core1",
 )
-PEERS = tuple((step, turn) for step in range(4) for turn in range(2))[1:]
-INDEX = {name: place for place, name in enumerate(NAMES)}
+def chunk_of(step, turn, half):
+    if turn:
+        return 3 + step * 2 + half
+    return {0: half * 15, 1: 1 + half, 3: 11 + half, 2: 13 + half}[step]
+
+
+OWN = (chunk_of(0, 0, 0), chunk_of(0, 0, 1))
+ACROSS = (chunk_of(0, 1, 0), chunk_of(0, 1, 1))
+INDEX = {name: place for place, name in enumerate(EARLY + tuple(n for n in NAMES if n not in EARLY))}
 
 
 def gelu_pair(preact):
@@ -49,7 +58,7 @@
     x_hbm, u_hbm, w_hbm, g_hbm, out_ref, ing_ref, du_hbm, dw_hbm,
     u_ref, w_ref, du_ref, dw_ref, local_sem,
     tok, pa, pb, ta, da, sa, ya_out, ya_in, ya_own, rb, tb, db, sb, ha, hb,
-    part, cr, zr, last_in, yo_out, yo_in, yo_own, acc_u, acc_w, send_sem, recv_sem, peer_sem, tok_sem,
+    part, cr, zr, yo_out, yo_in, acc_u, acc_w, send_sem, recv_sem, tok_sem, o_sem, y_sem,
 ):
     z0 = lax.axis_index("ia")
     ja = lax.axis_index("ja")
@@ -58,6 +67,7 @@
     h0, c0 = ka // 2, ka % 2
     rows = x_hbm.shape[1]
     last = CHUNKS - 1
+    halves = range(2)
 
     def at_x(step):
         return (z0, y0 * 4 + (x0 + step + 4) % 4, ka)
@@ -71,25 +81,38 @@
     ways = ((0, 1), (1, -1))
 
     barrier = pltpu.get_barrier_semaphore()
-    peers = [((z0 + step) % 4, ja, (h0 + turn) % 2 * 2 + c0) for step, turn in PEERS]
-    for other in [at_x(1), at_x(-1), y_pair, c_pair] + peers:
+    for other in (at_x(1), at_x(-1), y_pair, c_pair, h_pair, at_z(1), at_z(2), at_z(3)):
         pl.semaphore_signal(barrier, inc=1, device_id=other, device_id_type=MESH)
-    load_x = pltpu.make_async_copy(x_hbm, tok.at[0, :, c0, z0, h0], local_sem.at[4])
-    load_g = pltpu.make_async_copy(g_hbm, tok.at[1, :, c0, z0, h0], local_sem.at[5])
-    load_u = pltpu.make_async_copy(u_hbm, u_ref, local_sem.at[0])
-    load_w = pltpu.make_async_copy(w_hbm, w_ref, local_sem.at[1])
-    store_u = pltpu.make_async_copy(du_ref, du_hbm, local_sem.at[2])
-    store_w = pltpu.make_async_copy(dw_ref, dw_hbm, local_sem.at[3])
-    for one in (load_x, load_g, load_u, load_w):
+    loads = [
+        pltpu.make_async_copy(ref.at[half], tok.at[t, OWN[half], c0], local_sem.at[t, half])
+        for t, ref in enumerate((x_hbm, g_hbm)) for half in halves
+    ]
+    load_u = pltpu.make_async_copy(u_hbm, u_ref, local_sem.at[2, 0])
+    load_w = pltpu.make_async_copy(w_hbm, w_ref, local_sem.at[2, 1])
+    spans = (slice(None, WIDE), slice(WIDE, None))
+    store_u = [
+        pltpu.make_async_copy(du_ref.at[:, span], du_hbm.at[:, span], local_sem.at[3, number])
+        for number, span in enumerate(spans)
+    ]
+    store_w = [
+        pltpu.make_async_copy(dw_ref.at[span], dw_hbm.at[span], local_sem.at[4, number])
+        for number, span in enumerate(spans)
+    ]
+    for one in loads + [load_u, load_w]:
         one.start()
-    load_x.wait()
-    load_g.wait()
-    pl.semaphore_wait(barrier, 4 + len(PEERS))
+    for one in loads:
+        one.wait()
+    pl.semaphore_wait(barrier, 8)
 
     def copy(name, c, src, dst, to):
+        more = name in EARLY
+        sent, received = SENT + more, RECEIVED + more
+        place = INDEX[name]
+        skipped = 0 if more else len(EARLY)
         return pltpu.make_async_remote_copy(
             src_ref=src, dst_ref=dst,
-            send_sem=send_sem.at[INDEX[name], c % SENT], recv_sem=recv_sem.at[INDEX[name], c % RECEIVED],
+            send_sem=send_sem.at[place * sent + skipped + c % sent],
+            recv_sem=recv_sem.at[place * received + skipped + c % received],
             device_id=to, device_id_type=MESH,
         )
 
@@ -142,37 +165,28 @@
             )
         return totals
 
-    def tok_y(c):
-        here = tok.at[:, c, c0, z0, h0]
+    def chunk_copy(sem, c, src, dst, to):
         return pltpu.make_async_remote_copy(
-            src_ref=here, dst_ref=here, send_sem=tok_sem.at[0, c], recv_sem=tok_sem.at[1, c],
-            device_id=h_pair, device_id_type=MESH,
+            src_ref=src, dst_ref=dst, send_sem=sem.at[0, c], recv_sem=sem.at[1, c],
+            device_id=to, device_id_type=MESH,
         )
 
-    def tok_z(c):
-        here = tok.at[:, c, c0, z0]
-        return [copy(f"tok_z{step}", c, here, here, at_z(step)) for step in (1, 2, 3)]
-
-    def peer_copy(which, place, src, dst):
-        return pltpu.make_async_remote_copy(
-            src_ref=src, dst_ref=dst,
-            send_sem=peer_sem.at[which, 0, place], recv_sem=peer_sem.at[which, 1, place],
-            device_id=peers[place], device_id_type=MESH,
-        )
-
-    def first_tokens():
-        here = tok.at[:, 0, c0, z0, h0]
-        return [peer_copy(0, place, here, here) for place in range(len(PEERS))]
-
-    def last_sums():
-        return [
-            peer_copy(1, place, cr.at[last, :, (z0 + step) % 4, (h0 + turn) % 2], last_in.at[place])
-            for place, (step, turn) in enumerate(PEERS)
-        ]
-
-    def tok_core(c):
+    def tok_z(step, turn, half):
+        c = chunk_of(step, turn, half)
+        mine = (ACROSS if turn else OWN)[half]
+        return chunk_copy(tok_sem, c, tok.at[:, mine, c0], tok.at[:, c, c0], at_z(-step))
+
+    def tok_y(half):
+        c = ACROSS[half]
+        return chunk_copy(tok_sem, c, tok.at[:, OWN[half], c0], tok.at[:, c, c0], h_pair)
+
+    def tok_arrived(c):
         here = tok.at[:, c, c0]
-        return copy("tok_core", c, here, here, c_pair)
+        chunk_copy(tok_sem, c, here, here, h_pair).wait_recv()
+
+    def tok_core(c, t):
+        here = tok.at[t, c, c0]
+        return copy(f"tok_core{t}", c, here, here, c_pair)
 
     def a_piece(c, t, x):
         return pa.at[c % HELD, t, x]
@@ -186,11 +200,10 @@
         return copy("a_y", c, ya_out.at[s], ya_in.at[s], y_pair)
 
     def b_y(c, t):
-        s = c % SLOTS
-        return copy(f"b_y{t}", c, pb.at[c % HELD, t, 1 - y0], rb.at[s, t], y_pair)
+        return copy(f"b_y{t}", c, pb.at[c % HELD, t, 1 - y0], rb.at[c % PAIRED, t], y_pair)
 
     def b_piece(c, t, x):
-        return rb.at[c % SLOTS, t, x]
+        return rb.at[c % PAIRED, t, x]
 
     def b_args(c):
         s = c % SLOTS
@@ -226,13 +239,14 @@
         return copy(f"o_core{t}", c, part.at[c % HELD, t, 1 - c0], cr.at[c, t], c_pair)
 
     def o_z(c):
-        return [
-            copy(f"o_z{step}", c, cr.at[c, :, (z0 + step) % 4], zr.at[c, step - 1], at_z(step))
-            for step in (1, 2, 3)
-        ]
-
-    def o_y(c):
-        return copy("o_y", c, yo_out.at[c % SLOTS], yo_in.at[c], h_pair)
+        step = jnp.where(c < 3, 1, jnp.where(c < 11, (c - 3) // 2, 3 - (c - 11) // 2))
+        return chunk_copy(o_sem, c, cr.at[c], zr.at[c], ((z0 + step) % 4, ja, ka))
+
+    def o_y():
+        return pltpu.make_async_remote_copy(
+            src_ref=yo_out, dst_ref=yo_in, send_sem=y_sem.at[0], recv_sem=y_sem.at[1],
+            device_id=h_pair, device_id_type=MESH,
+        )
 
     def start(copies):
         for one in copies:
@@ -247,25 +261,17 @@
     def wide(c, t):
         return tok[t, c].reshape(-1, tok.shape[-1])
 
-    def gather_tokens(c):
-        finish((tok_y(c),))
-        start(tok_z(c))
-
     def gather_tokens_core(c):
-        @pl.when(c > 0)
+        @pl.when((c != OWN[1]) & (c != ACROSS[0]) & (c != ACROSS[1]))
         def _():
-            finish(tok_z(c))
-
-        @pl.when(c == 0)
-        def _():
-            finish(first_tokens())
-
-        start((tok_core(c),))
+            tok_arrived(c)
+
+        start([tok_core(c, t) for t in range(2)])
 
     def multiply_in(c):
-        finish((tok_core(c),))
         s = c % HELD
         for t, way in ways:
+            finish((tok_core(c, t),))
             if t == 0:
                 both = contract(wide(c, 0), u_ref[...], ((1,), (0,)))
             else:
@@ -283,7 +289,8 @@
         piece, transit, direct, _, mine, to = b_args(c)
         for t, way in ways:
             b_y(c, t).wait_recv()
-            rb[s, t] = (rb[s, t].astype(F32) + pb[c % HELD, t, y0].astype(F32)).astype(BF16)
+            here = rb.at[c % PAIRED, t]
+            here[...] = (here[...].astype(F32) + pb[c % HELD, t, y0].astype(F32)).astype(BF16)
             start(sum_first("b", c, t, way, piece, transit, direct, mine, to))
         for t in range(2):
             b_y(c, t).wait_send()
@@ -348,9 +355,28 @@
             o_core(c, t).start()
 
     def add_grads(c):
-        for cols, src in ((slice(None, WIDE), ha), (slice(WIDE, None), hb)):
-            acc_u[:, cols] += contract(wide(c, 0), src[1, c].reshape(-1, src.shape[-1]), ((0,), (0,)))
-            acc_w[cols] += contract(src[0, c].reshape(-1, src.shape[-1]), wide(c, 1), ((0,), (0,)))
+        def add(flat):
+            for span, src in zip(spans, (ha, hb)):
+                acc_u[:, span] += contract(flat(tok, 0), flat(src, 1), ((0,), (0,)))
+                acc_w[span] += contract(flat(src, 0), flat(tok, 1), ((0,), (0,)))
+
+        @pl.when((c % 2 == 1) & (c < last))
+        def _():
+            add(lambda ref, t: ref[t, pl.ds(c - 1, 2)].reshape(-1, ref.shape[-1]))
+
+        @pl.when(c == last - 1)
+        def _():
+            add(lambda ref, t: ref[t, c].reshape(-1, ref.shape[-1]))
+
+    def finish_grads():
+        def flat(ref, t):
+            return ref[t, last].reshape(-1, ref.shape[-1])
+
+        for number, (span, src) in enumerate(zip(spans, (ha, hb))):
+            dw_ref[span] = (acc_w[span] + contract(flat(src, 0), flat(tok, 1), ((0,), (0,)))).astype(BF16)
+            store_w[number].start()
+            du_ref[:, span] = (acc_u[:, span] + contract(flat(tok, 0), flat(src, 1), ((0,), (0,)))).astype(BF16)
+            store_u[number].start()
 
     def total_one(c):
         s = c % HELD
@@ -358,62 +384,48 @@
             finish((o_core(c, t),))
             cr[c, t] = (cr[c, t].astype(F32) + part[s, t, c0].astype(F32)).astype(BF16)
 
-        @pl.when(c < last)
+    def total_two(c):
+        total_one(c)
+
+        @pl.when((c != OWN[0]) & (c != ACROSS[0]) & (c != ACROSS[1]))
         def _():
-            start(o_z(c))
-
-        @pl.when(c == last)
-        def _():
-            start(last_sums())
-
-    def total_two(c):
-        s = c % SLOTS
-
-        @pl.when(c < last)
-        def _():
-            finish(o_z(c))
+            o_z(c).start()
+
+    def sum_parts(first, chunks, t):
+        total = first.astype(F32)
+        for c in chunks:
+            total += zr[c, t].astype(F32)
+        return total
+
+    def total_across():
+        for half in halves:
+            chunks = [chunk_of(step, 1, half) for step in (1, 2, 3)]
+            for c in chunks:
+                o_z(c).wait_recv()
             for t in range(2):
-                first, second = (
-                    cr[c, t, z0, h].astype(F32) + zr[c, 0, t, h].astype(F32)
-                    + zr[c, 1, t, h].astype(F32) + zr[c, 2, t, h].astype(F32)
-                    for h in range(2)
-                )
-                yo_own[s, t] = jnp.where(h0 == 0, first, second)
-                yo_out[s, t] = jnp.where(h0 == 0, second, first).astype(BF16)
-            o_y(c).start()
-
-        @pl.when(c == last)
-        def _():
-            du_ref[...] = acc_u[...].astype(BF16)
-            store_u.start()
-            dw_ref[...] = acc_w[...].astype(BF16)
-            store_w.start()
-            finish(last_sums())
+                yo_out[half, t] = sum_parts(cr[ACROSS[half], t], chunks, t).astype(BF16)
+        o_y().start()
+
+    def total_own():
+        o_y().wait_recv()
+        for half in halves:
+            chunks = [chunk_of(step, 0, half) for step in (1, 3, 2)]
+            for c in chunks:
+                o_z(c).wait_recv()
+            at = slice(half * rows, (half + 1) * rows)
             for t, ref in enumerate((out_ref, ing_ref)):
-                total = cr[c, t, z0, h0].astype(F32)
-                for place in range(len(PEERS)):
-                    total += last_in[place, t].astype(F32)
-                ref[last * rows:, :] = total.astype(BF16)
-
-    def total_three(c):
-        s = c % SLOTS
-
-        @pl.when(c < last)
-        def _():
-            finish((o_y(c),))
-            at = pl.ds(pl.multiple_of(c * rows, rows), rows)
-            out_ref[at, :] = (yo_own[s, 0] + yo_in[c, 0].astype(F32)).astype(BF16)
-            ing_ref[at, :] = (yo_own[s, 1] + yo_in[c, 1].astype(F32)).astype(BF16)
+                total = sum_parts(cr[OWN[half], t], chunks, t) + yo_in[half, t].astype(F32)
+                ref[at, :] = total.astype(BF16)
 
     stages = (
-        (10, total_three), (9, total_two), (8, total_one), (7, multiply_out), (6, gather_two),
-        (5, gather_one), (4, activate), (3, sum_two), (2, sum_one), (1, multiply_in),
-        (0, gather_tokens_core), (-1, gather_tokens), (8, add_grads),
+        (9, total_two), (8, multiply_out), (7, gather_two), (6, gather_one), (5, activate),
+        (4, sum_two), (3, sum_one), (1, multiply_in), (0, gather_tokens_core), (8, add_grads),
     )
 
-    start(first_tokens())
-    for c in range(1, CHUNKS):
-        tok_y(c).start()
+    start([tok_core(0, t) for t in range(2)])
+    start([tok_z(1, 0, half) for half in halves])
+    start([tok_y(half) for half in halves])
+    start([tok_z(step, 0, half) for step in (3, 2) for half in halves])
     acc_u[...] = jnp.zeros_like(acc_u)
     acc_w[...] = jnp.zeros_like(acc_w)
     load_u.wait()
@@ -421,14 +433,38 @@
 
     def step(number, carry):
         for behind, stage in stages:
-            @pl.when((number >= behind) & (number < behind + CHUNKS))
+            begin = 1 if stage is gather_tokens_core else behind
+
+            @pl.when((number >= begin) & (number < behind + CHUNKS))
             def _():
                 stage(number - behind)
+
+        @pl.when(number == 2)
+        def _():
+            for half in halves:
+                tok_arrived(ACROSS[half])
+                start([tok_z(other, 1, half) for other in (1, 2, 3)])
+
+        @pl.when(number == chunk_of(3, 1, 1) + 11)
+        def _():
+            total_across()
+
         return carry
 
-    lax.fori_loop(0, CHUNKS + 9, step, 0)
-    store_u.wait()
-    store_w.wait()
+    lax.fori_loop(0, CHUNKS + 8, step, 0)
+    finish_grads()
+    total_one(last)
+    total_own()
+    for half in halves:
+        tok_y(half).wait_send()
+        for other in (1, 2, 3):
+            tok_z(other, 0, half).wait_send()
+            tok_z(other, 1, half).wait_send()
+            o_z(chunk_of(other, 0, half)).wait_send()
+            o_z(chunk_of(other, 1, half)).wait_send()
+    o_y().wait_send()
+    for one in store_u + store_w:
+        one.wait()
 
 
 def hand_on(*refs):
@@ -456,8 +492,8 @@
 def per_device(inputs, up_weight, down_weight, out_grad):
     tokens, width = inputs.shape
     hidden = up_weight.shape[1]
-    rows = tokens // CHUNKS
-    owned = rows * 2
+    rows = tokens // 2
+    owned = rows // 4
     narrow = hidden - WIDE
 
     def vmem(*shape, dtype=BF16):
@@ -468,31 +504,29 @@
         vmem(hidden, width),
         vmem(width, hidden),
         vmem(hidden, width),
-        pltpu.SemaphoreType.DMA((6,)),
-        vmem(2, CHUNKS, 2, 4, 2, rows, width),
+        pltpu.SemaphoreType.DMA((5, 2)),
+        vmem(2, CHUNKS, 2, rows, width),
         vmem(HELD, 2, 4, 2, owned, WIDE),
         vmem(HELD, 2, 2, 4, owned, narrow),
         *[vmem(SLOTS, 2, 2, owned, WIDE)] * 3,
         vmem(SLOTS, 2, owned, WIDE),
         vmem(SLOTS, 2, owned, WIDE),
         vmem(SLOTS, 2, owned, WIDE, dtype=F32),
-        vmem(SLOTS, 2, 4, owned, narrow),
+        vmem(PAIRED, 2, 4, owned, narrow),
         *[vmem(SLOTS, 2, owned, narrow)] * 3,
         vmem(2, CHUNKS, 4, 2, owned, WIDE),
         vmem(2, CHUNKS, 2, 4, owned, narrow),
-        vmem(HELD, 2, 2, 4, 2, rows, width),
-        vmem(CHUNKS, 2, 4, 2, rows, width),
-        vmem(CHUNKS, 3, 2, 2, rows, width),
-        vmem(len(PEERS), 2, rows, width),
-        vmem(SLOTS, 2, rows, width),
+        vmem(HELD, 2, 2, rows, width),
         vmem(CHUNKS, 2, rows, width),
-        vmem(SLOTS, 2, rows, width, dtype=F32),
+        vmem(CHUNKS, 2, rows, width),
+        vmem(2, 2, rows, width),
+        vmem(2, 2, rows, width),
         vmem(width, hidden, dtype=F32),
         vmem(hidden, width, dtype=F32),
-        pltpu.SemaphoreType.DMA((len(NAMES), SENT)),
-        pltpu.SemaphoreType.DMA((len(NAMES), RECEIVED)),
-        pltpu.SemaphoreType.DMA((2, 2, len(PEERS))),
-        pltpu.SemaphoreType.DMA((2, CHUNKS)),
+        pltpu.SemaphoreType.DMA((len(NAMES) * SENT + len(EARLY),)),
+        pltpu.SemaphoreType.DMA((len(NAMES) * RECEIVED + len(EARLY),)),
+        *[pltpu.SemaphoreType.DMA((2, CHUNKS))] * 2,
+        pltpu.SemaphoreType.DMA((2,)),
     ]
     results = (
         jax.ShapeDtypeStruct(inputs.shape, BF16),
@@ -511,8 +545,8 @@
             collective_id=0, has_side_effects=True, vmem_limit_bytes=62 * 1024 * 1024
         ),
     )(
-        inputs.reshape(CHUNKS, rows, width), up_weight, down_weight,
-        out_grad.reshape(CHUNKS, rows, width),
+        inputs.reshape(2, rows, width), up_weight, down_weight,
+        out_grad.reshape(2, rows, width),
     )
     return pl.pallas_call(
         hand_on,

time: 208 us -> 197 us (0.947)
  Pallas kernels: 207 us -> 197 us
    pallas_call x1, Pallas kernels: 203 us -> 192 us  [per_device(): pl.pallas_call(kernel, out_shape=results, in_specs=[far] * 4, out_specs=[...]
where the time goes in v5:
time: 197 us
  Pallas kernels  197 us (100%)
    pallas_call x1, Pallas kernels, per_device(): pl.pallas_call(kernel, out_shape=results, in_specs=[far] * 4, out_specs=[...  192 us
    pallas_call x1, Pallas kernels, per_device(): pl.pallas_call(hand_on, out_shape=results, in_specs=[far] * 4, out_specs=...  4.22 us

profile of v5, /device:TPU:0, one launch (start us, length us, event | category | flops | bytes accessed | tf_op | source)
XLA Modules:
  0.0 197.3 jit_solution(2493168409592228184)
XLA Ops:
  0.6 192.5 %shard_map.75 = (bf16[128,768]{1,0:T(8,128)(2,1)}, bf16[128,768]{1,0:T(8,128)(2,1)}, bf16[768,1536]{1,0:T(8,128)(2,1)}, bf16[1536,768]{1,0:T(8,128)(2,1)}) custom-call(bf16[2,64,768]{2,1,0:T(8,128)(2,1)} %bitcast.2, bf16[768,1536]{1,0:T(8,128)(2,1)} %u_hbm.1, bf16[1536,768]{1,0:T(8,128)(2,1)} %w_hbm.1, bf16[2,64,768]{2,1,0:T(8,128)(2,1)} %bitcast.3), custom_call_target="tpu_custom_call" | custom-call | tf_op jit(solution)/shard_map/pallas_call | solution.py:538
  193.1 4.2 %shard_map.76 = (bf16[128,768]{1,0:T(8,128)(2,1)}, bf16[128,768]{1,0:T(8,128)(2,1)}, bf16[768,1536]{1,0:T(8,128)(2,1)}, bf16[1536,768]{1,0:T(8,128)(2,1)}) custom-call(bf16[128,768]{1,0:T(8,128)(2,1)} %get-tuple-element.8.refs_0_, bf16[128,768]{1,0:T(8,128)(2,1)} %get-tuple-element.9.refs_1_, bf16[768,1536]{1,0:T(8,128)(2,1)} %get-tuple-element.10.refs_2_, ...), custom_call_target="tpu_custom_call" | custom-call | tf_op jit(solution)/shard_map/pallas_call | solution.py:551

commit v6 on v5

--- a/solution.py
+++ b/solution.py
@@ -34,7 +34,7 @@
 def chunk_of(step, turn, half):
     if turn:
         return 3 + step * 2 + half
-    return {0: half * 15, 1: 1 + half, 3: 11 + half, 2: 13 + half}[step]
+    return {0: half * 15, 1: 1 + half, 2: 11 + half, 3: 13 + half}[step]
 
 
 OWN = (chunk_of(0, 0, 0), chunk_of(0, 0, 1))
@@ -58,7 +58,7 @@
     x_hbm, u_hbm, w_hbm, g_hbm, out_ref, ing_ref, du_hbm, dw_hbm,
     u_ref, w_ref, du_ref, dw_ref, local_sem,
     tok, pa, pb, ta, da, sa, ya_out, ya_in, ya_own, rb, tb, db, sb, ha, hb,
-    part, cr, zr, yo_out, yo_in, acc_u, acc_w, send_sem, recv_sem, tok_sem, o_sem, y_sem,
+    part, cr, zr, yo_out, yo_in, acc_u, acc_w, send_sem, recv_sem, tok_sem, o_sem, y_sem, far_sem,
 ):
     z0 = lax.axis_index("ia")
     ja = lax.axis_index("ja")
@@ -235,11 +235,26 @@
     def gb_second(c):
         return gather_second("gb", c, lambda t, x: hb.at[t, c, y0, x], x0, at_x, "x")
 
+    def far_copy(number, src):
+        return pltpu.make_async_remote_copy(
+            src_ref=src, dst_ref=src, send_sem=far_sem.at[0, number], recv_sem=far_sem.at[1, number],
+            device_id=at_x(2), device_id_type=MESH,
+        )
+
+    def ga_far():
+        return far_copy(0, ha.at[:, last, x0, y0])
+
+    def gp_far():
+        return far_copy(1, ha.at[:, last, x0, 1 - y0])
+
+    def gb_far():
+        return far_copy(2, hb.at[:, last, y0, x0])
+
     def o_core(c, t):
         return copy(f"o_core{t}", c, part.at[c % HELD, t, 1 - c0], cr.at[c, t], c_pair)
 
     def o_z(c):
-        step = jnp.where(c < 3, 1, jnp.where(c < 11, (c - 3) // 2, 3 - (c - 11) // 2))
+        step = jnp.where(c < 3, 1, jnp.where(c < 11, (c - 3) // 2, 2 + (c - 11) // 2))
         return chunk_copy(o_sem, c, cr.at[c], zr.at[c], ((z0 + step) % 4, ja, ka))
 
     def o_y():
@@ -320,15 +335,41 @@
         gb_y(c, 0).start()
         start(gb_first(c))
 
+        @pl.when(c == last)
+        def _():
+            start((ga_far(), gb_far()))
+
     def gather_one(c):
         finish((ga_y(c),))
         start(gp_first(c))
+
+        @pl.when(c == last)
+        def _():
+            gp_far().start()
+
         finish(gb_first(c))
-        start(gb_second(c))
+
+        @pl.when(c < last)
+        def _():
+            start(gb_second(c))
+
         start((gb_y(c, 1), gb_y(c, 3)))
+
+        @pl.when(c == last)
+        def _():
+            finish((gb_far(),))
+            gb_y(c, 2).start()
+
         finish((gb_y(c, 0),))
         finish(ga_first(c))
-        start(ga_second(c))
+
+        @pl.when(c < last)
+        def _():
+            start(ga_second(c))
+
+        @pl.when(c == last)
+        def _():
+            finish((ga_far(),))
 
     def gather_two(c):
         finish(gp_first(c))
@@ -341,6 +382,15 @@
         finish(ga_second(c))
         finish(gp_second(c))
         finish((gb_y(c, 2),))
+        multiply_gathered(c)
+
+    def multiply_last():
+        finish(gp_first(last))
+        finish((gp_far(),))
+        finish([gb_y(last, step) for step in (1, 2, 3)])
+        multiply_gathered(last)
+
+    def multiply_gathered(c):
         s = c % HELD
         for t in range(2):
             left_a = ha[t, c].reshape(-1, ha.shape[-1])
@@ -409,7 +459,7 @@
     def total_own():
         o_y().wait_recv()
         for half in halves:
-            chunks = [chunk_of(step, 0, half) for step in (1, 3, 2)]
+            chunks = [chunk_of(step, 0, half) for step in (1, 2, 3)]
             for c in chunks:
                 o_z(c).wait_recv()
             at = slice(half * rows, (half + 1) * rows)
@@ -425,7 +475,7 @@
     start([tok_core(0, t) for t in range(2)])
     start([tok_z(1, 0, half) for half in halves])
     start([tok_y(half) for half in halves])
-    start([tok_z(step, 0, half) for step in (3, 2) for half in halves])
+    start([tok_z(step, 0, half) for step in (2, 3) for half in halves])
     acc_u[...] = jnp.zeros_like(acc_u)
     acc_w[...] = jnp.zeros_like(acc_w)
     load_u.wait()
@@ -435,7 +485,9 @@
         for behind, stage in stages:
             begin = 1 if stage is gather_tokens_core else behind
 
-            @pl.when((number >= begin) & (number < behind + CHUNKS))
+            count = CHUNKS - 1 if stage is gather_two else CHUNKS
+
+            @pl.when((number >= begin) & (number < behind + count))
             def _():
                 stage(number - behind)
 
@@ -451,7 +503,9 @@
 
         return carry
 
-    lax.fori_loop(0, CHUNKS + 8, step, 0)
+    lax.fori_loop(0, CHUNKS + 7, step, 0)
+    total_two(last - 1)
+    multiply_last()
     finish_grads()
     total_one(last)
     total_own()
@@ -527,6 +581,7 @@
         pltpu.SemaphoreType.DMA((len(NAMES) * RECEIVED + len(EARLY),)),
         *[pltpu.SemaphoreType.DMA((2, CHUNKS))] * 2,
         pltpu.SemaphoreType.DMA((2,)),
+        pltpu.SemaphoreType.DMA((2, 3)),
     ]
     results = (
         jax.ShapeDtypeStruct(inputs.shape, BF16),

time: 197 us -> 195 us (0.990)
  Pallas kernels: 197 us -> 194 us
    pallas_call x1, Pallas kernels: 192 us -> 190 us  [per_device(): pl.pallas_call(kernel, out_shape=results, in_specs=[far] * 4, out_specs=[...]
where the time goes in v6:
time: 195 us
  Pallas kernels  194 us (99%)
    pallas_call x1, Pallas kernels, per_device(): pl.pallas_call(kernel, out_shape=results, in_specs=[far] * 4, out_specs=[...  190 us
    pallas_call x1, Pallas kernels, per_device(): pl.pallas_call(hand_on, out_shape=results, in_specs=[far] * 4, out_specs=...  4.22 us

profile of v6, /device:TPU:0, one launch (start us, length us, event | category | flops | bytes accessed | tf_op | source)
XLA Modules:
  0.0 194.9 jit_solution(11636894623444066652)
XLA Ops:
  0.6 190.1 %shard_map.75 = (bf16[128,768]{1,0:T(8,128)(2,1)}, bf16[128,768]{1,0:T(8,128)(2,1)}, bf16[768,1536]{1,0:T(8,128)(2,1)}, bf16[1536,768]{1,0:T(8,128)(2,1)}) custom-call(bf16[2,64,768]{2,1,0:T(8,128)(2,1)} %bitcast.2, bf16[768,1536]{1,0:T(8,128)(2,1)} %u_hbm.1, bf16[1536,768]{1,0:T(8,128)(2,1)} %w_hbm.1, bf16[2,64,768]{2,1,0:T(8,128)(2,1)} %bitcast.3), custom_call_target="tpu_custom_call" | custom-call | tf_op jit(solution)/shard_map/pallas_call | solution.py:593
  190.7 4.2 %shard_map.76 = (bf16[128,768]{1,0:T(8,128)(2,1)}, bf16[128,768]{1,0:T(8,128)(2,1)}, bf16[768,1536]{1,0:T(8,128)(2,1)}, bf16[1536,768]{1,0:T(8,128)(2,1)}) custom-call(bf16[128,768]{1,0:T(8,128)(2,1)} %get-tuple-element.8.refs_0_, bf16[128,768]{1,0:T(8,128)(2,1)} %get-tuple-element.9.refs_1_, bf16[768,1536]{1,0:T(8,128)(2,1)} %get-tuple-element.10.refs_2_, ...), custom_call_target="tpu_custom_call" | custom-call | tf_op jit(solution)/shard_map/pallas_call | solution.py:606

commit v7 on v6

--- a/solution.py
+++ b/solution.py
@@ -277,11 +277,15 @@
         return tok[t, c].reshape(-1, tok.shape[-1])
 
     def gather_tokens_core(c):
-        @pl.when((c != OWN[1]) & (c != ACROSS[0]) & (c != ACROSS[1]))
+        @pl.when(c != OWN[1])
         def _():
             tok_arrived(c)
 
         start([tok_core(c, t) for t in range(2)])
+        for half in halves:
+            @pl.when(c == ACROSS[half])
+            def _():
+                start([tok_z(other, 1, half) for other in (1, 2, 3)])
 
     def multiply_in(c):
         s = c % HELD
@@ -490,12 +494,6 @@
             @pl.when((number >= begin) & (number < behind + count))
             def _():
                 stage(number - behind)
-
-        @pl.when(number == 2)
-        def _():
-            for half in halves:
-                tok_arrived(ACROSS[half])
-                start([tok_z(other, 1, half) for other in (1, 2, 3)])
 
         @pl.when(number == chunk_of(3, 1, 1) + 11)
         def _():

time: 195 us -> 195 us (level)
  no operation moved by 1% of the time
where the time goes in v7:
time: 195 us
  Pallas kernels  194 us (99%)
    pallas_call x1, Pallas kernels, per_device(): pl.pallas_call(kernel, out_shape=results, in_specs=[far] * 4, out_specs=[...  190 us
    pallas_call x1, Pallas kernels, per_device(): pl.pallas_call(hand_on, out_shape=results, in_specs=[far] * 4, out_specs=...  4.22 us

profile of v7, /device:TPU:0, one launch (start us, length us, event | category | flops | bytes accessed | tf_op | source)
XLA Modules:
  0.0 195.0 jit_solution(3402417641024904157)
XLA Ops:
  0.6 190.1 %shard_map.75 = (bf16[128,768]{1,0:T(8,128)(2,1)}, bf16[128,768]{1,0:T(8,128)(2,1)}, bf16[768,1536]{1,0:T(8,128)(2,1)}, bf16[1536,768]{1,0:T(8,128)(2,1)}) custom-call(bf16[2,64,768]{2,1,0:T(8,128)(2,1)} %bitcast.2, bf16[768,1536]{1,0:T(8,128)(2,1)} %u_hbm.1, bf16[1536,768]{1,0:T(8,128)(2,1)} %w_hbm.1, bf16[2,64,768]{2,1,0:T(8,128)(2,1)} %bitcast.3), custom_call_target="tpu_custom_call" | custom-call | tf_op jit(solution)/shard_map/pallas_call | solution.py:591
  190.8 4.2 %shard_map.76 = (bf16[128,768]{1,0:T(8,128)(2,1)}, bf16[128,768]{1,0:T(8,128)(2,1)}, bf16[768,1536]{1,0:T(8,128)(2,1)}, bf16[1536,768]{1,0:T(8,128)(2,1)}) custom-call(bf16[128,768]{1,0:T(8,128)(2,1)} %get-tuple-element.8.refs_0_, bf16[128,768]{1,0:T(8,128)(2,1)} %get-tuple-element.9.refs_1_, bf16[768,1536]{1,0:T(8,128)(2,1)} %get-tuple-element.10.refs_2_, ...), custom_call_target="tpu_custom_call" | custom-call | tf_op jit(solution)/shard_map/pallas_call | solution.py:604
